TPU v7x, 256 devices: a whole 4x4x8 slice. The times are simulated.
256 devices in a mesh: grp: 16 (over z, core), dev: 16 (over y, x).
Axes of the slice: x: 4, y: 4, z: 8, core: 2. Of those that a mesh axis runs over, the one named last changes fastest.
Arguments:
- features: bfloat16 [3072, 512, 128], P(('grp', 'dev')), may hold values from -6 to 6
- occupancy: int32 [3072, 512], P(('grp', 'dev')), may hold values 0 or 1
- w_first: bfloat16 [27, 128, 128], replicated, may hold values from -0.125 to 0.125
- w_second: bfloat16 [27, 128, 128], replicated, may hold values from -0.125 to 0.125
- src_ref: int32 [3072, 27], P(('grp', 'dev')), may hold values from -1 to 31, as said below
- send_list: int32 [256, 16, 1], P(('grp', 'dev')), may hold values from -1 to 11, as said below
Outputs:
- block_out: bfloat16 [3072, 512, 128], P(('grp', 'dev'))
Inputs may be any that keep to these rules, and one draw needn't show every extreme that they name: Entry src_ref[b, 13] is b's own position among its device's bricks. Entries 0 to 11 are the device's own bricks, the next 2 the lower end set, the next 2 the upper one, then one slot for each device p of the coarse range in order of p. No entry refers to an end set that does not exist or to a slot whose send_list entry is -1; every slot that carries a brick is referred to by some entry of the receiving device. `send_list`: A device sends nothing to itself; in every coarse range, each device receives one brick from the device just after it in its range, counted cyclically.
All inputs are finite; a program needn't handle non-finite values. No bound on the sum of `occupancy` on one device may be relied on, other than what follows from the above.
Results may differ from a plain program's by a relative error of at most 0.0031.
Values may be sent and summed in bfloat16 or wider, within the bound.
No kernel may reach another device: no remote copies, remote signals or barrier semaphores. Data moves between devices by JAX's collectives and lax.ppermute only.
A program may use at most 128 MiB of HBM per device.

v0:
```python
import functools

import jax
import jax.numpy as jnp
import numpy as np
from jax import lax
from jax.experimental import pallas as pl
from jax.experimental.pallas import tpu as pltpu
from jax.sharding import PartitionSpec as P

BR = 12
EDGE = 2
SLOTS = 16
ENTRIES = BR + 2 * EDGE + SLOTS
BLANK = ENTRIES
SHELL = 304
FACE_LO = 224
FACE_HI = 260
MIB = 1024 * 1024
LIMIT = 62


def ring_row(x, y):
    if x == 0:
        return y * 8
    if x == 7:
        return 64 + y * 8
    if y == 0:
        return 128 + (x - 1) * 8
    if y == 7:
        return 176 + (x - 1) * 8
    return None


def cell_row(x, y, z):
    first = ring_row(x, y)
    if first is not None:
        return first + z
    return (FACE_LO if z == 0 else FACE_HI) + (x - 1) * 6 + (y - 1)


def shell_matrix():
    picked = np.zeros((SHELL, 512), np.float32)
    for x in range(8):
        for y in range(8):
            for z in range(8):
                cell = x * 64 + y * 8 + z
                first = ring_row(x, y)
                if first is not None:
                    picked[first + z, cell] = 1
                elif z in (0, 7):
                    picked[cell_row(x, y, z), cell] = 1
    return jnp.asarray(picked, jnp.bfloat16)


def start_all(copies):
    for copy in copies:
        copy.start()
    return copies


def wait_all(copies):
    for copy in copies:
        copy.wait()


def hand_out(send_ref, own, out_ref, low_ref, high_ref, sems):
    copies = [pltpu.make_async_copy(own.at[:EDGE], high_ref, sems.at[SLOTS])]
    copies.append(pltpu.make_async_copy(own.at[BR - EDGE :], low_ref, sems.at[SLOTS + 1]))
    for slot in range(SLOTS):
        brick = jnp.maximum(send_ref[slot], 0)
        copies.append(pltpu.make_async_copy(own.at[brick], out_ref.at[slot], sems.at[slot]))
    return start_all(copies)


def pack_kernel(
    send_ref, feat_ref, occ_ref, pick_ref, out_ref, low_ref, high_ref, feats, own, in_sems, out_sems
):
    pairs = [pl.ds(pair * 2, 2) for pair in range(BR // 2)]
    loads = start_all(
        [pltpu.make_async_copy(feat_ref.at[at], feats.at[at], in_sems.at[n]) for n, at in enumerate(pairs)]
    )
    for pair, load in enumerate(loads):
        load.wait()
        for brick in (2 * pair, 2 * pair + 1):
            held = occ_ref[brick : brick + 1, :].astype(jnp.float32).astype(jnp.bfloat16)
            chooser = pick_ref[...] * jnp.broadcast_to(held, (SHELL, 512))
            shell = jnp.dot(chooser, feats[brick], preferred_element_type=jnp.float32)
            own[brick] = shell.astype(jnp.bfloat16)
    wait_all(hand_out(send_ref, own, out_ref, low_ref, high_ref, out_sems))


def toeplitz(target, taps):
    t0, t1, t2 = taps
    zero = jnp.zeros((128, 128), jnp.bfloat16)
    target[0, 0:128, 0:128] = t0
    target[0, 0:128, 128:256] = zero
    target[0, 128:256, 0:128] = t1
    target[0, 128:256, 128:256] = t0
    target[1, 0:128, 0:128] = t2
    target[1, 0:128, 128:256] = t1
    target[1, 128:256, 0:128] = zero
    target[1, 128:256, 128:256] = t2


def edge_masks():
    sub = lax.broadcasted_iota(jnp.int32, (8, 128), 0)
    return sub == 0, sub == 7


def shift_down(value, first, fill):
    return jnp.where(first, fill, pltpu.roll(value, 1, 0))


def shift_up(value, last, fill):
    return jnp.where(last, fill, pltpu.roll(value, 7, 0))


def own_conv(plane, w_ref, part_ref, wide, block, base=None):
    step = pl.program_id(0)

    @pl.when(step == 0)
    def _():
        block[...] = jnp.zeros_like(block)
        for tap in range(9):
            toeplitz(wide.at[tap], (w_ref[tap], w_ref[9 + tap], w_ref[18 + tap]))

    first, last = edge_masks()
    for x in range(8):
        planes = [plane(half, x) for half in range(2)]
        px = x + 1
        lanes = slice((px % 2) * 128, (px % 2) * 128 + 128)
        for y in range(8):
            mids = [planes[half][y * 8 : y * 8 + 8] for half in range(2)]
            for az, parts in enumerate(
                (
                    [shift_down(mid, first, 0.0) for mid in mids],
                    mids,
                    [shift_up(mid, last, 0.0) for mid in mids],
                )
            ):
                block[az, px // 2, y + 1, :, lanes] = jnp.concatenate(parts, axis=0).astype(jnp.bfloat16)
    acc = jnp.zeros((512, 256), jnp.float32)
    for az in range(3):
        for ay in range(3):
            for side in range(2):
                part = block[az, side : side + 4, ay : ay + 8].reshape(512, 256)
                acc = acc + jnp.dot(part, wide[ay * 3 + az, side], preferred_element_type=jnp.float32)
    if base is None:
        part_ref[0] = acc
        return
    for half in range(2):
        for x in range(8):
            added = base(half, x)
            lanes = slice((x % 2) * 128, (x % 2) * 128 + 128)
            for y in range(8):
                row = (x // 2) * 128 + y * 16 + half * 8
                part_ref[0, row : row + 8, lanes] = acc[row : row + 8, lanes] + added[y * 8 : y * 8 + 8]


def first_own_kernel(feat_ref, occ_ref, pick_ref, w_ref, part_ref, x_ref, mask_ref, shell_ref, wide, block):
    step = pl.program_id(0)
    rows = lax.broadcasted_iota(jnp.int32, (128, 128), 0)
    cols = lax.broadcasted_iota(jnp.int32, (128, 128), 1)
    diagonal = rows == cols
    ones = jnp.ones((128, 128), jnp.bfloat16)
    held = {}
    for half in range(2):
        occupied = occ_ref[pl.ds(step * 2 + half, 1), :].astype(jnp.float32)
        for chunk in range(4):
            cells = slice(chunk * 128, chunk * 128 + 128)
            scale = jnp.where(diagonal, jnp.broadcast_to(occupied[:, cells], (128, 128)), 0.0).astype(jnp.bfloat16)
            right = jnp.concatenate([feat_ref[half, cells, :], ones], axis=1)
            both = jnp.dot(scale, right, preferred_element_type=jnp.float32)
            x_ref[half, cells, :] = both[:, :128].astype(jnp.bfloat16)
            mask_ref[half, cells, :] = both[:, 128:].astype(jnp.bfloat16)
            held[half, 2 * chunk] = both[:64, :128]
            held[half, 2 * chunk + 1] = both[64:, :128]
        shell = jnp.dot(pick_ref[...], x_ref[half], preferred_element_type=jnp.float32)
        shell_ref[half] = shell.astype(jnp.bfloat16)
    own_conv(lambda half, x: held[half, x], w_ref, part_ref, wide, block)


def second_own_kernel(hidden_ref, x_ref, pick_ref, w_ref, part_ref, shell_ref, wide, block):
    for half in range(2):
        shell = jnp.dot(pick_ref[...], hidden_ref[half], preferred_element_type=jnp.float32)
        shell_ref[half] = shell.astype(jnp.bfloat16)
    plane = lambda ref: lambda half, x: ref[half, x * 64 : x * 64 + 64, :].astype(jnp.float32)
    own_conv(plane(hidden_ref), w_ref, part_ref, wide, block, plane(x_ref))


def fill_pool(pool, start, source):
    for entry in range(source.shape[0]):
        pool[start + entry] = source[entry].astype(jnp.float32)


def build_halos(pair, src_ref, pool, halo):
    first, last = edge_masks()
    entries = []
    for half in range(2):
        refs = [src_ref[pair * 2 + half, k] for k in range(27)]
        entries.append([jnp.where(r < 0, BLANK, r) for r in refs])
    at = pl.ds(pl.multiple_of(pair * 16, 16), 16)

    def put(face, outer, parts):
        lanes = slice((outer % 2) * 128, (outer % 2) * 128 + 128)
        for shift in range(3):
            both = jnp.concatenate([parts[0][shift], parts[1][shift]], axis=0)
            halo[face, shift, outer // 2, at, lanes] = both.astype(jnp.bfloat16)

    def column(half, base, x, y):
        below, here, above = (entries[half][base + dz] for dz in range(3))
        start, at_lo, at_hi = ring_row(x, y), cell_row(x, y, 7), cell_row(x, y, 0)
        mid = pool[here, start : start + 8, :]
        lo = jnp.broadcast_to(pool[below, at_lo : at_lo + 1, :], (8, 128))
        hi = jnp.broadcast_to(pool[above, at_hi : at_hi + 1, :], (8, 128))
        return shift_down(mid, first, lo), mid, shift_up(mid, last, hi)

    for face, (delta, cell, z_cell) in enumerate(((0, 7, 7), (2, 0, 0))):
        for outer in range(10):
            dy = 0 if outer == 0 else (2 if outer == 9 else 1)
            y = 7 if outer == 0 else (0 if outer == 9 else outer - 1)
            put(face, outer, [column(half, delta * 9 + dy * 3, cell, y) for half in range(2)])
        for x in range(8):
            put(2 + face, x + 1, [column(half, 9 + delta * 3, x, cell) for half in range(2)])
        for x in range(8):
            parts = []
            for half in range(2):
                entry = entries[half][12 + delta]
                if x in (0, 7):
                    mid = pool[entry, pl.ds(ring_row(x, 0) + z_cell, 8, stride=8), :]
                else:
                    start = cell_row(x, 1, z_cell) - 1
                    at_lo, at_hi = cell_row(x, 0, z_cell), cell_row(x, 7, z_cell)
                    mid = pool[entry, start : start + 8, :]
                    mid = jnp.where(first, jnp.broadcast_to(pool[entry, at_lo : at_lo + 1, :], (8, 128)), mid)
                    mid = jnp.where(last, jnp.broadcast_to(pool[entry, at_hi : at_hi + 1, :], (8, 128)), mid)
                parts.append((shift_down(mid, first, 0.0), mid, shift_up(mid, last, 0.0)))
            put(4 + face, x + 1, parts)


def halo_weights(w_ref, along):
    for face in range(2):
        end = 2 * face
        for shift in range(3):
            toeplitz(along.at[face, shift], [w_ref[end * 9 + tap * 3 + shift] for tap in range(3)])
            toeplitz(along.at[2 + face, shift], [w_ref[tap * 9 + end * 3 + shift] for tap in range(3)])
            toeplitz(along.at[4 + face, shift], [w_ref[tap * 9 + shift * 3 + end] for tap in range(3)])


def halo_sums(halo, along, sums):
    rows = 8 * BR
    for face in range(6):
        acc = jnp.zeros((4 * rows, 256), jnp.float32)
        for shift in range(3):
            for side in range(2):
                part = halo[face, shift, side : side + 4].reshape(4 * rows, 256)
                acc = acc + jnp.dot(part, along[face, shift, side], preferred_element_type=jnp.float32)
        sums[face] = acc.reshape(4, BR, 8, 256)


def halo_part(src_ref, sources, landed, sems, streams, stream_sems, pool, halo, along, sums):
    loads = start_all([pltpu.make_async_copy(a, b, sems.at[n]) for n, (a, b) in enumerate(zip(sources, landed))])
    for n, (source, target, size) in enumerate(streams):
        for pair in range(BR // 2):
            at = pl.ds(pair * size, size)
            pltpu.make_async_copy(source.at[at], target.at[at], stream_sems.at[n, pair]).start()
    pool[BLANK] = jnp.zeros((SHELL, 128), jnp.float32)
    for face in range(2, 6):
        for shift in range(3):
            halo[face, shift, 0, :, 0:128] = jnp.zeros((8 * BR, 128), jnp.bfloat16)
            halo[face, shift, 4, :, 128:256] = jnp.zeros((8 * BR, 128), jnp.bfloat16)
    loads[0].wait()
    halo_weights(landed[0], along)
    for load, start, field in zip(loads[1:], (0, BR, BR + EDGE, BR + 2 * EDGE), landed[1:]):
        load.wait()
        fill_pool(pool, start, field)

    def pair_body(pair, carry):
        build_halos(pair, src_ref, pool, halo)
        return carry

    lax.fori_loop(0, BR // 2, pair_body, 0)
    halo_sums(halo, along, sums)


def wait_stream(streams, stream_sems, pair):
    for n, (source, target, size) in enumerate(streams):
        at = pl.ds(pair * size, size)
        pltpu.make_async_copy(source.at[at], target.at[at], stream_sems.at[n, pair]).wait()


def whole_plane(part, sums, pair, half, x):
    first, last = edge_masks()
    brick = pair * 2 + half
    lanes = slice((x % 2) * 128, (x % 2) * 128 + 128)
    columns = []
    for y in range(8):
        row = (x // 2) * 128 + y * 16 + half * 8
        value = part[pair, row : row + 8, lanes]
        if x in (0, 7):
            value = value + sums[x // 7, y // 2, brick, :, (y % 2) * 128 : (y % 2) * 128 + 128]
        if y in (0, 7):
            value = value + sums[2 + y // 7, x // 2, brick, :, lanes]
        lo = jnp.broadcast_to(sums[4, x // 2, brick, y : y + 1, lanes], (8, 128))
        hi = jnp.broadcast_to(sums[5, x // 2, brick, y : y + 1, lanes], (8, 128))
        columns.append(value + jnp.where(first, lo, jnp.where(last, hi, 0.0)))
    return jnp.concatenate(columns, axis=0)


def first_halo_kernel(
    src_ref, send_ref, pick_ref, part_ref, mask_ref, w_ref, shells_ref, before_ref, after_ref, recv_ref,
    hidden_ref, out_ref, low_ref, high_ref,
    pool, halo, along, sums, w, shells, before, after, recv, part, mask, done, sems, stream_sems, done_sems,
    own, out_sems,
):
    streams = ((part_ref, part, 1), (mask_ref, mask, 2))
    sources = (w_ref, shells_ref, before_ref, after_ref, recv_ref)
    landed = (w, shells, before, after, recv)
    halo_part(src_ref, sources, landed, sems, streams, stream_sems, pool, halo, along, sums)

    def store(pair):
        at = pl.ds(pair * 2, 2)
        return pltpu.make_async_copy(done.at[at], hidden_ref.at[at], done_sems.at[pair])

    def pair_body(pair, carry):
        wait_stream(streams, stream_sems, pair)
        for half in range(2):
            brick = pair * 2 + half
            for x in range(8):
                rows = slice(x * 64, x * 64 + 64)
                value = whole_plane(part, sums, pair, half, x)
                value = value / (1.0 + jnp.exp(-value)) * mask[brick, rows, :].astype(jnp.float32)
                done[brick, rows, :] = value.astype(jnp.bfloat16)
            shell = jnp.dot(pick_ref[...], done[brick], preferred_element_type=jnp.float32)
            own[brick] = shell.astype(jnp.bfloat16)
        store(pair).start()
        return carry

    lax.fori_loop(0, BR // 2, pair_body, 0)
    copies = hand_out(send_ref, own, out_ref, low_ref, high_ref, out_sems)
    wait_all([store(pair) for pair in range(BR // 2)])
    wait_all(copies)


def second_halo_kernel(
    src_ref, part_ref, mask_ref, w_ref, shells_ref, before_ref, after_ref, recv_ref,
    result_ref,
    pool, halo, along, sums, w, shells, before, after, recv, part, mask, done, sems, stream_sems, done_sems,
):
    streams = ((part_ref, part, 1), (mask_ref, mask, 2))
    sources = (w_ref, shells_ref, before_ref, after_ref, recv_ref)
    landed = (w, shells, before, after, recv)
    halo_part(src_ref, sources, landed, sems, streams, stream_sems, pool, halo, along, sums)

    def store(pair):
        at = pl.ds(pair * 2, 2)
        return pltpu.make_async_copy(done.at[at], result_ref.at[at], done_sems.at[pair])

    def pair_body(pair, carry):
        wait_stream(streams, stream_sems, pair)
        for half in range(2):
            brick = pair * 2 + half
            for x in range(8):
                rows = slice(x * 64, x * 64 + 64)
                value = whole_plane(part, sums, pair, half, x)
                done[brick, rows, :] = (value * mask[brick, rows, :].astype(jnp.float32)).astype(jnp.bfloat16)
        store(pair).start()
        return carry

    lax.fori_loop(0, BR // 2, pair_body, 0)
    wait_all([store(pair) for pair in range(BR // 2)])


WHOLE = functools.partial(pl.BlockSpec, memory_space=pltpu.VMEM)
SCALARS = functools.partial(pl.BlockSpec, memory_space=pltpu.SMEM)
ANYWHERE = functools.partial(pl.BlockSpec, memory_space=pl.ANY)
GRID = (BR // 2,)
FIELD = jax.ShapeDtypeStruct((BR, 512, 128), jnp.bfloat16)
PARTIAL = jax.ShapeDtypeStruct((BR // 2, 512, 256), jnp.float32)


def pair_spec():
    return pl.BlockSpec((2, 512, 128), lambda i: (i, 0, 0))


def part_spec():
    return pl.BlockSpec((1, 512, 256), lambda i: (i, 0, 0))


def shell_pair_spec():
    return pl.BlockSpec((2, SHELL, 128), lambda i: (i, 0, 0))


def shells_of(*counts):
    return [jax.ShapeDtypeStruct((n, SHELL, 128), jnp.bfloat16) for n in counts]


def params(mib):
    return pltpu.CompilerParams(vmem_limit_bytes=mib * MIB)


def own_scratch():
    return [pltpu.VMEM((9, 2, 256, 256), jnp.bfloat16), pltpu.VMEM((3, 5, 10, 16, 256), jnp.bfloat16)]


def halo_scratch():
    shells = [pltpu.VMEM((n, SHELL, 128), jnp.bfloat16) for n in (BR, EDGE, EDGE, SLOTS)]
    return [
        pltpu.VMEM((ENTRIES + 1, SHELL, 128), jnp.float32),
        pltpu.VMEM((6, 3, 5, 8 * BR, 256), jnp.bfloat16),
        pltpu.VMEM((6, 3, 2, 256, 256), jnp.bfloat16),
        pltpu.VMEM((6, 4, BR, 8, 256), jnp.float32),
        pltpu.VMEM((27, 128, 128), jnp.bfloat16),
        *shells,
        pltpu.VMEM((BR // 2, 512, 256), jnp.float32),
        pltpu.VMEM((BR, 512, 128), jnp.bfloat16),
        pltpu.VMEM((BR, 512, 128), jnp.bfloat16),
        pltpu.SemaphoreType.DMA((5,)),
        pltpu.SemaphoreType.DMA((2, BR // 2)),
        pltpu.SemaphoreType.DMA((BR // 2,)),
    ]


def own_shells_scratch():
    return [pltpu.VMEM((BR, SHELL, 128), jnp.bfloat16), pltpu.SemaphoreType.DMA((SLOTS + 2,))]


OWN_COST = pl.CostEstimate(flops=2 * 6 * 512 * 4608 * 256, bytes_accessed=8 * MIB, transcendentals=0)
HALO_COST = pl.CostEstimate(flops=2 * 36 * 384 * 256 * 256, bytes_accessed=10 * MIB, transcendentals=0)


def pack(send, feats, occ, pick):
    return pl.pallas_call(
        pack_kernel,
        in_specs=[SCALARS(), ANYWHERE(), WHOLE(), WHOLE()],
        out_specs=[ANYWHERE()] * 3,
        out_shape=shells_of(SLOTS, EDGE, EDGE),
        scratch_shapes=[
            pltpu.VMEM((BR, 512, 128), jnp.bfloat16),
            pltpu.VMEM((BR, SHELL, 128), jnp.bfloat16),
            pltpu.SemaphoreType.DMA((BR // 2,)),
            pltpu.SemaphoreType.DMA((SLOTS + 2,)),
        ],
        compiler_params=params(LIMIT),
        name="pack_shells",
    )(send, feats, occ, pick)


def first_own(feats, occ, pick, weights):
    return pl.pallas_call(
        first_own_kernel,
        grid=GRID,
        in_specs=[pair_spec(), WHOLE(), WHOLE(), WHOLE()],
        out_specs=[part_spec(), pair_spec(), pair_spec(), shell_pair_spec()],
        out_shape=[PARTIAL, FIELD, FIELD] + shells_of(BR),
        scratch_shapes=own_scratch(),
        compiler_params=params(LIMIT),
        cost_estimate=OWN_COST,
        name="first_own",
    )(feats, occ, pick, weights)


def second_own(hidden, x, pick, weights):
    return pl.pallas_call(
        second_own_kernel,
        grid=GRID,
        in_specs=[pair_spec(), pair_spec(), WHOLE(), WHOLE()],
        out_specs=[part_spec(), shell_pair_spec()],
        out_shape=[PARTIAL] + shells_of(BR),
        scratch_shapes=own_scratch(),
        compiler_params=params(LIMIT),
        cost_estimate=OWN_COST,
        name="second_own",
    )(hidden, x, pick, weights)


def first_halo(src, send, pick, part, mask, weights, shells, before, after, recv):
    return pl.pallas_call(
        first_halo_kernel,
        in_specs=[SCALARS(), SCALARS(), WHOLE()] + [ANYWHERE()] * 7,
        out_specs=[ANYWHERE()] * 4,
        out_shape=[FIELD] + shells_of(SLOTS, EDGE, EDGE),
        scratch_shapes=halo_scratch() + own_shells_scratch(),
        compiler_params=params(LIMIT),
        cost_estimate=HALO_COST,
        name="first_halo",
    )(src, send, pick, part, mask, weights, shells, before, after, recv)


def second_halo(src, part, mask, weights, shells, before, after, recv):
    return pl.pallas_call(
        second_halo_kernel,
        in_specs=[SCALARS()] + [ANYWHERE()] * 7,
        out_specs=ANYWHERE(),
        out_shape=FIELD,
        scratch_shapes=halo_scratch(),
        compiler_params=params(LIMIT),
        cost_estimate=HALO_COST,
        name="second_halo",
    )(src, part, mask, weights, shells, before, after, recv)


def shifted(value, axis, steps):
    count = lax.axis_size(axis)
    initial, last = (max(0, -steps), min(count, count - steps))
    return lax.ppermute(value, axis, [(source, source + steps) for source in range(initial, last)])


def exchange(outgoing, low, high):
    arrived = lax.all_to_all(outgoing, "dev", split_axis=0, concat_axis=0, tiled=True)
    before = shifted(low, ("grp", "dev"), 1)
    after = shifted(high, ("grp", "dev"), -1)
    return before, after, arrived


def per_device(features, occupancy, w_first, w_second, src_ref, send_list):
    send = send_list.reshape(SLOTS)
    pick = shell_matrix()
    outgoing, low, high = pack(send, features, occupancy, pick)
    around = exchange(outgoing, low, high)
    part, x, mask, shells = first_own(features, occupancy, pick, w_first)
    hidden, outgoing, low, high = first_halo(src_ref, send, pick, part, mask, w_first, shells, *around)
    around = exchange(outgoing, low, high)
    part, shells = second_own(hidden, x, pick, w_second)
    return second_halo(src_ref, part, mask, w_second, shells, *around)


def solution(mesh):
    placed = (
        P(("grp", "dev"), None, None),
        P(("grp", "dev"), None),
        P(),
        P(),
        P(("grp", "dev"), None),
        P(("grp", "dev"), None, None),
    )
    return jax.shard_map(
        per_device,
        mesh=mesh,
        in_specs=placed,
        out_specs=P(("grp", "dev"), None, None),
        check_vma=False,
    )
```

profile of v0, /device:TPU:128, one launch (start us, length us, event | category | flops | bytes accessed | tf_op | source)
XLA Modules:
  0.0 90.5 jit_solution(523892153716671666)
XLA Ops:
  0.0 5.3 %pack_shells.1 = (bf16[16,304,128]{2,1,0:T(8,128)(2,1)}, bf16[2,304,128]{2,1,0:T(8,128)(2,1)}, bf16[2,304,128]{2,1,0:T(8,128)(2,1)}) custom-call(s32[16]{0:T(128)} %bitcast.1, bf16[12,512,128]{2,1,0:T(8,128)(2,1)} %feat_ref.3, s32[12,512]{1,0:T(8,128)} %occ_ref.3, bf16[304,512]{1,0:T(8,128)(2,1)} %constant.2.clone.pick_ref), custom_call_target="tpu_custom_call" | custom-call | tf_op jit(solution)/shard_map/pack_shells/pallas_call | solution.py:434
  5.3 0.0 copy-start.9
  5.3 0.0 copy-start.8
  5.3 7.2 %all-to-all-start = ((bf16[16,304,128]{2,1,0:T(8,128)(2,1)}), bf16[16,304,128]{2,1,0:T(8,128)(2,1)S(1)}, u32[]{:S(2)}, u32[]{:S(2)}) async-start(bf16[16,304,128]{2,1,0:T(8,128)(2,1)} %get-tuple-element.23), calls=%async_computation | async-start | bytes 2490368 | tf_op jit(solution)/shard_map/all_to_all | solution.py:511
  12.5 0.0 copy-done.9
  12.5 3.8 %collective-permute-start = (bf16[2,304,128]{2,1,0:T(8,128)(2,1)S(1)}, bf16[2,304,128]{2,1,0:T(8,128)(2,1)S(1)}, u32[]{:S(2)}, u32[]{:S(2)}) collective-permute-start(bf16[2,304,128]{2,1,0:T(8,128)(2,1)S(1)} %copy-done.9), channel_id=1, source_target_pairs={{0,1},{1,2},{2,3},{3,4},{4,5},{5,6},{6,7},{7,8},{8,9},{9,10},{10,1... | collective-permute-start | bytes 466952 | tf_op jit(solution)/shard_map/ppermute | solution.py:507
  16.3 0.0 copy-done.8
  16.3 7.2 %collective-permute-start.1 = (bf16[2,304,128]{2,1,0:T(8,128)(2,1)S(1)}, bf16[2,304,128]{2,1,0:T(8,128)(2,1)S(1)}, u32[]{:S(2)}, u32[]{:S(2)}) collective-permute-start(bf16[2,304,128]{2,1,0:T(8,128)(2,1)S(1)} %copy-done.8), channel_id=1, source_target_pairs={{1,0},{2,1},{3,2},{4,3},{5,4},{6,5},{7,6},{8,7},{9,8},{10,9},{11,1... | collective-permute-start | bytes 466952 | tf_op jit(solution)/shard_map/ppermute | solution.py:507
  23.5 15.3 %first_own.1 = (f32[6,512,256]{2,1,0:T(8,128)}, bf16[12,512,128]{2,1,0:T(8,128)(2,1)}, bf16[12,512,128]{2,1,0:T(8,128)(2,1)}, bf16[12,304,128]{2,1,0:T(8,128)(2,1)}) custom-call(bf16[12,512,128]{2,1,0:T(8,128)(2,1)} %feat_ref.3, s32[12,512]{1,0:T(8,128)} %occ_ref.3, bf16[304,512]{1,0:T(8,128)(2,1)} %constant.2.clone.pick_ref, bf16[27,128,128]{2,1,0:T(8,128)(2,1)} %w_ref.5), custom_call_target="tpu_custom_call" | custom-call | flops 7247757312 | bytes 8388608 | tf_op jit(solution)/shard_map/first_own/pallas_call | solution.py:451
  38.8 0.0 collective-permute-done.before_ref
  38.8 0.0 copy-start.2
  38.8 0.0 collective-permute-done.1.after_ref
  38.8 0.0 copy-start.3
  38.8 0.0 all-to-all-done.recv_ref
  38.8 0.0 copy-start
  38.8 0.6 copy-done.2
  39.5 0.1 copy-done.3
  39.5 0.5 copy-done
  40.0 12.0 %first_halo.1 = (bf16[12,512,128]{2,1,0:T(8,128)(2,1)}, bf16[16,304,128]{2,1,0:T(8,128)(2,1)}, bf16[2,304,128]{2,1,0:T(8,128)(2,1)}, bf16[2,304,128]{2,1,0:T(8,128)(2,1)}) custom-call(s32[12,27]{1,0:T(8,128)} %src_ref.3, s32[16]{0:T(128)} %bitcast.2, bf16[304,512]{1,0:T(8,128)(2,1)} %constant.2.clone.pick_ref, f32[6,512,256]{2,1,0:T(8,128)} %get-tuple-element.18.part_ref, ...), custom_call_target="tpu_custom_call" | custom-call | flops 1811939328 | bytes 10485760 | tf_op jit(solution)/shard_map/first_halo/pallas_call | solution.py:479
  52.1 0.0 copy-start.7
  52.1 0.0 copy-start.6
  52.1 3.8 %all-to-all-start.1 = ((bf16[16,304,128]{2,1,0:T(8,128)(2,1)}), bf16[16,304,128]{2,1,0:T(8,128)(2,1)S(1)}, u32[]{:S(2)}, u32[]{:S(2)}) async-start(bf16[16,304,128]{2,1,0:T(8,128)(2,1)} %get-tuple-element.30), calls=%async_computation.1 | async-start | bytes 2490368 | tf_op jit(solution)/shard_map/all_to_all | solution.py:511
  55.9 0.0 copy-done.7
  55.9 3.7 %collective-permute-start.2 = (bf16[2,304,128]{2,1,0:T(8,128)(2,1)S(1)}, bf16[2,304,128]{2,1,0:T(8,128)(2,1)S(1)}, u32[]{:S(2)}, u32[]{:S(2)}) collective-permute-start(bf16[2,304,128]{2,1,0:T(8,128)(2,1)S(1)} %copy-done.7), channel_id=1, source_target_pairs={{0,1},{1,2},{2,3},{3,4},{4,5},{5,6},{6,7},{7,8},{8,9},{9,10},{10,1... | collective-permute-start | bytes 466952 | tf_op jit(solution)/shard_map/ppermute | solution.py:507
  59.7 0.0 copy-done.6
  59.7 7.5 %collective-permute-start.3 = (bf16[2,304,128]{2,1,0:T(8,128)(2,1)S(1)}, bf16[2,304,128]{2,1,0:T(8,128)(2,1)S(1)}, u32[]{:S(2)}, u32[]{:S(2)}) collective-permute-start(bf16[2,304,128]{2,1,0:T(8,128)(2,1)S(1)} %copy-done.6), channel_id=1, source_target_pairs={{1,0},{2,1},{3,2},{4,3},{5,4},{6,5},{7,6},{8,7},{9,8},{10,9},{11,1... | collective-permute-start | bytes 466952 | tf_op jit(solution)/shard_map/ppermute | solution.py:507
  67.1 13.1 %second_own.1 = (f32[6,512,256]{2,1,0:T(8,128)}, bf16[12,304,128]{2,1,0:T(8,128)(2,1)}) custom-call(bf16[12,512,128]{2,1,0:T(8,128)(2,1)} %get-tuple-element.24.hidden_ref, bf16[12,512,128]{2,1,0:T(8,128)(2,1)} %get-tuple-element.25.x_ref, bf16[304,512]{1,0:T(8,128)(2,1)} %constant.2.clone.pick_ref, bf16[27,128,128]{2,1,0:T(8,128)(2,1)} %w_ref.7), custom_call_target="tpu_custom_call" | custom-call | flops 7247757312 | bytes 8388608 | tf_op jit(solution)/shard_map/second_own/pallas_call | solution.py:465
  80.2 0.0 collective-permute-done.2.before_ref
  80.2 0.0 copy-start.4
  80.3 0.0 collective-permute-done.3.after_ref
  80.3 0.0 copy-start.5
  80.3 0.0 all-to-all-done.1.recv_ref
  80.3 0.0 copy-start.1
  80.3 0.6 copy-done.4
  80.9 0.1 copy-done.5
  81.0 0.4 copy-done.1
  81.4 8.9 %second_halo.1 = bf16[12,512,128]{2,1,0:T(8,128)(2,1)} custom-call(s32[12,27]{1,0:T(8,128)} %src_ref.3, f32[6,512,256]{2,1,0:T(8,128)} %get-tuple-element.26.part_ref, bf16[12,512,128]{2,1,0:T(8,128)(2,1)} %get-tuple-element.19.mask_ref, bf16[27,128,128]{2,1,0:T(8,128)(2,1)} %w_ref.7, bf16[12,304,128]{2,1,0:T(8,128)(2,1)} %get-tuple-element.27.shells_ref, ...), custom_call_target="tpu_custom_call" | custom-call | flops 1811939328 | bytes 10485760 | tf_op jit(solution)/shard_map/second_halo/pallas_call | solution.py:492
Async XLA Ops:
  5.3 7.2 %copy-start.9 = (bf16[2,304,128]{2,1,0:T(8,128)(2,1)S(1)}, bf16[2,304,128]{2,1,0:T(8,128)(2,1)}, u32[]{:S(2)}) copy-start(bf16[2,304,128]{2,1,0:T(8,128)(2,1)} %get-tuple-element.21) | copy-start | bytes 466948
  5.3 11.0 %copy-start.8 = (bf16[2,304,128]{2,1,0:T(8,128)(2,1)S(1)}, bf16[2,304,128]{2,1,0:T(8,128)(2,1)}, u32[]{:S(2)}) copy-start(bf16[2,304,128]{2,1,0:T(8,128)(2,1)} %get-tuple-element.22) | copy-start | bytes 466948
  5.3 33.5 %all-to-all-start = ((bf16[16,304,128]{2,1,0:T(8,128)(2,1)}), bf16[16,304,128]{2,1,0:T(8,128)(2,1)S(1)}, u32[]{:S(2)}, u32[]{:S(2)}) async-start(bf16[16,304,128]{2,1,0:T(8,128)(2,1)} %get-tuple-element.23), calls=%async_computation | async-start | bytes 2490368 | tf_op jit(solution)/shard_map/all_to_all | solution.py:511
  12.5 26.3 %collective-permute-start = (bf16[2,304,128]{2,1,0:T(8,128)(2,1)S(1)}, bf16[2,304,128]{2,1,0:T(8,128)(2,1)S(1)}, u32[]{:S(2)}, u32[]{:S(2)}) collective-permute-start(bf16[2,304,128]{2,1,0:T(8,128)(2,1)S(1)} %copy-done.9), channel_id=1, source_target_pairs={{0,1},{1,2},{2,3},{3,4},{4,5},{5,6},{6,7},{7,8},{8,9},{9,10},{10,1... | collective-permute-start | bytes 466952 | tf_op jit(solution)/shard_map/ppermute | solution.py:507
  16.3 22.5 %collective-permute-start.1 = (bf16[2,304,128]{2,1,0:T(8,128)(2,1)S(1)}, bf16[2,304,128]{2,1,0:T(8,128)(2,1)S(1)}, u32[]{:S(2)}, u32[]{:S(2)}) collective-permute-start(bf16[2,304,128]{2,1,0:T(8,128)(2,1)S(1)} %copy-done.8), channel_id=1, source_target_pairs={{1,0},{2,1},{3,2},{4,3},{5,4},{6,5},{7,6},{8,7},{9,8},{10,9},{11,1... | collective-permute-start | bytes 466952 | tf_op jit(solution)/shard_map/ppermute | solution.py:507
  38.8 0.7 copy-start.2
  38.8 0.7 copy-start.3
  38.8 1.2 %copy-start = (bf16[16,304,128]{2,1,0:T(8,128)(2,1)}, bf16[16,304,128]{2,1,0:T(8,128)(2,1)S(1)}, u32[]{:S(2)}) copy-start(bf16[16,304,128]{2,1,0:T(8,128)(2,1)S(1)} %all-to-all-done.recv_ref) | copy-start | bytes 3735556
  52.1 3.9 %copy-start.7 = (bf16[2,304,128]{2,1,0:T(8,128)(2,1)S(1)}, bf16[2,304,128]{2,1,0:T(8,128)(2,1)}, u32[]{:S(2)}) copy-start(bf16[2,304,128]{2,1,0:T(8,128)(2,1)} %get-tuple-element.28) | copy-start | bytes 466948
  52.1 7.6 %copy-start.6 = (bf16[2,304,128]{2,1,0:T(8,128)(2,1)S(1)}, bf16[2,304,128]{2,1,0:T(8,128)(2,1)}, u32[]{:S(2)}) copy-start(bf16[2,304,128]{2,1,0:T(8,128)(2,1)} %get-tuple-element.29) | copy-start | bytes 466948
  52.1 28.2 %all-to-all-start.1 = ((bf16[16,304,128]{2,1,0:T(8,128)(2,1)}), bf16[16,304,128]{2,1,0:T(8,128)(2,1)S(1)}, u32[]{:S(2)}, u32[]{:S(2)}) async-start(bf16[16,304,128]{2,1,0:T(8,128)(2,1)} %get-tuple-element.30), calls=%async_computation.1 | async-start | bytes 2490368 | tf_op jit(solution)/shard_map/all_to_all | solution.py:511
  55.9 24.3 %collective-permute-start.2 = (bf16[2,304,128]{2,1,0:T(8,128)(2,1)S(1)}, bf16[2,304,128]{2,1,0:T(8,128)(2,1)S(1)}, u32[]{:S(2)}, u32[]{:S(2)}) collective-permute-start(bf16[2,304,128]{2,1,0:T(8,128)(2,1)S(1)} %copy-done.7), channel_id=1, source_target_pairs={{0,1},{1,2},{2,3},{3,4},{4,5},{5,6},{6,7},{7,8},{8,9},{9,10},{10,1... | collective-permute-start | bytes 466952 | tf_op jit(solution)/shard_map/ppermute | solution.py:507
  59.7 20.6 %collective-permute-start.3 = (bf16[2,304,128]{2,1,0:T(8,128)(2,1)S(1)}, bf16[2,304,128]{2,1,0:T(8,128)(2,1)S(1)}, u32[]{:S(2)}, u32[]{:S(2)}) collective-permute-start(bf16[2,304,128]{2,1,0:T(8,128)(2,1)S(1)} %copy-done.6), channel_id=1, source_target_pairs={{1,0},{2,1},{3,2},{4,3},{5,4},{6,5},{7,6},{8,7},{9,8},{10,9},{11,1... | collective-permute-start | bytes 466952 | tf_op jit(solution)/shard_map/ppermute | solution.py:507
  80.2 0.7 copy-start.4
  80.3 0.7 copy-start.5
  80.3 1.1 %copy-start.1 = (bf16[16,304,128]{2,1,0:T(8,128)(2,1)}, bf16[16,304,128]{2,1,0:T(8,128)(2,1)S(1)}, u32[]{:S(2)}) copy-start(bf16[16,304,128]{2,1,0:T(8,128)(2,1)S(1)} %all-to-all-done.1.recv_ref) | copy-start | bytes 3735556
where the time goes:
time: 91 us; the launch traced here: 90.5 us
  Pallas kernels  54.6 us (60%)
  starting transfers between devices  33.2 us (36%)
  local copies, waits for them, and re-layouts  2.33 us (3%)
    ppermute x4, starting transfers between devices, shifted(): lax.ppermute(value, axis, [(source, source + steps) for source in range(i...  22.2 us
    pallas_call x1, Pallas kernels, first_own(): pl.pallas_call(first_own_kernel, grid=GRID, in_specs=[pair_spec(), WHOLE(...  15.3 us
    pallas_call x1, Pallas kernels, second_own(): pl.pallas_call(second_own_kernel, grid=GRID, in_specs=[pair_spec(), pair_...  13.1 us
    pallas_call x1, Pallas kernels, first_halo(): pl.pallas_call(first_halo_kernel, in_specs=[SCALARS(), SCALARS(), WHOLE()...  12 us
    all_to_all x2, starting transfers between devices, exchange(): lax.all_to_all(outgoing, 'dev', split_axis=0, concat_axis=0, tiled=True)  11 us
    pallas_call x1, Pallas kernels, second_halo(): pl.pallas_call(second_halo_kernel, in_specs=[SCALARS()] + [ANYWHERE()] *...  8.89 us
    pallas_call x1, Pallas kernels, pack(): pl.pallas_call(pack_kernel, in_specs=[SCALARS(), ANYWHERE(), WHOLE(), WHO...  5.26 us
    unnamed x20, local copies, waits for them, and re-layouts  2.33 us
  transfers between devices with their start and end apart: 6, of which 0 were waited for; matrix products, arithmetic and copies ran while one was open for 0% of the time, Pallas kernels for 31%

commit v1 on v0

--- a/solution.py
+++ b/solution.py
@@ -17,7 +17,7 @@
 FACE_LO = 224
 FACE_HI = 260
 MIB = 1024 * 1024
-LIMIT = 62
+VMEM_LIMIT = 64 * MIB - 96 * 1024
 
 
 def ring_row(x, y):
@@ -53,6 +53,18 @@
     return jnp.asarray(picked, jnp.bfloat16)
 
 
+def store_shell(shell, planes, cells=None, pick=None):
+    shell[0:64, :] = planes[0].astype(jnp.bfloat16)
+    shell[64:128, :] = planes[7].astype(jnp.bfloat16)
+    for x in (1, 3, 5):
+        for start, rows in ((128, slice(0, 8)), (176, slice(56, 64))):
+            both = jnp.concatenate([planes[x][rows], planes[x + 1][rows]], axis=0)
+            shell[start + (x - 1) * 8 : start + (x + 1) * 8, :] = both.astype(jnp.bfloat16)
+    if cells is not None:
+        inner = jnp.dot(pick, cells, preferred_element_type=jnp.float32)
+        shell[FACE_LO:SHELL, :] = inner.astype(jnp.bfloat16)
+
+
 def start_all(copies):
     for copy in copies:
         copy.start()
@@ -74,17 +86,20 @@
 
 
 def pack_kernel(
-    send_ref, feat_ref, occ_ref, pick_ref, out_ref, low_ref, high_ref, feats, own, in_sems, out_sems
+    send_ref, feat_ref, occ_ref, pick_ref, out_ref, low_ref, high_ref, feats, own, pick, in_sems, out_sems
 ):
+    pick_load = pltpu.make_async_copy(pick_ref, pick, in_sems.at[BR // 2])
+    pick_load.start()
     pairs = [pl.ds(pair * 2, 2) for pair in range(BR // 2)]
     loads = start_all(
         [pltpu.make_async_copy(feat_ref.at[at], feats.at[at], in_sems.at[n]) for n, at in enumerate(pairs)]
     )
-    for pair, load in enumerate(loads):
-        load.wait()
-        for brick in (2 * pair, 2 * pair + 1):
+    pick_load.wait()
+    for part in range(0, BR // 2, 3):
+        wait_all(loads[part : part + 3])
+        for brick in range(2 * part, 2 * part + 6):
             held = occ_ref[brick : brick + 1, :].astype(jnp.float32).astype(jnp.bfloat16)
-            chooser = pick_ref[...] * jnp.broadcast_to(held, (SHELL, 512))
+            chooser = pick[...] * jnp.broadcast_to(held, (SHELL, 512))
             shell = jnp.dot(chooser, feats[brick], preferred_element_type=jnp.float32)
             own[brick] = shell.astype(jnp.bfloat16)
     wait_all(hand_out(send_ref, own, out_ref, low_ref, high_ref, out_sems))
@@ -176,16 +191,15 @@
             mask_ref[half, cells, :] = both[:, 128:].astype(jnp.bfloat16)
             held[half, 2 * chunk] = both[:64, :128]
             held[half, 2 * chunk + 1] = both[64:, :128]
-        shell = jnp.dot(pick_ref[...], x_ref[half], preferred_element_type=jnp.float32)
-        shell_ref[half] = shell.astype(jnp.bfloat16)
+        store_shell(shell_ref.at[half], [held[half, x] for x in range(8)], x_ref[half], pick_ref[...])
     own_conv(lambda half, x: held[half, x], w_ref, part_ref, wide, block)
 
 
 def second_own_kernel(hidden_ref, x_ref, pick_ref, w_ref, part_ref, shell_ref, wide, block):
+    plane = lambda ref: lambda half, x: ref[half, x * 64 : x * 64 + 64, :].astype(jnp.float32)
     for half in range(2):
-        shell = jnp.dot(pick_ref[...], hidden_ref[half], preferred_element_type=jnp.float32)
-        shell_ref[half] = shell.astype(jnp.bfloat16)
-    plane = lambda ref: lambda half, x: ref[half, x * 64 : x * 64 + 64, :].astype(jnp.float32)
+        planes = [plane(hidden_ref)(half, x) for x in range(8)]
+        store_shell(shell_ref.at[half], planes, hidden_ref[half], pick_ref[...])
     own_conv(plane(hidden_ref), w_ref, part_ref, wide, block, plane(x_ref))
 
 
@@ -194,49 +208,55 @@
         pool[start + entry] = source[entry].astype(jnp.float32)
 
 
-def build_halos(pair, src_ref, pool, halo):
+def build_face(face, src_ref, pool, halo):
     first, last = edge_masks()
-    entries = []
-    for half in range(2):
-        refs = [src_ref[pair * 2 + half, k] for k in range(27)]
-        entries.append([jnp.where(r < 0, BLANK, r) for r in refs])
-    at = pl.ds(pl.multiple_of(pair * 16, 16), 16)
-
-    def put(face, outer, parts):
+    delta, cell, z_cell = ((0, 7, 7), (2, 0, 0))[face % 2]
+
+    def entry(brick, k):
+        ref = src_ref[brick, k]
+        return jnp.where(ref < 0, BLANK, ref)
+
+    def put(pair, outer, parts):
         lanes = slice((outer % 2) * 128, (outer % 2) * 128 + 128)
         for shift in range(3):
             both = jnp.concatenate([parts[0][shift], parts[1][shift]], axis=0)
-            halo[face, shift, outer // 2, at, lanes] = both.astype(jnp.bfloat16)
-
-    def column(half, base, x, y):
-        below, here, above = (entries[half][base + dz] for dz in range(3))
+            halo[face, shift, outer // 2, pair * 16 : pair * 16 + 16, lanes] = both.astype(jnp.bfloat16)
+
+    def column(around, x, y):
+        below, here, above = around
         start, at_lo, at_hi = ring_row(x, y), cell_row(x, y, 7), cell_row(x, y, 0)
         mid = pool[here, start : start + 8, :]
         lo = jnp.broadcast_to(pool[below, at_lo : at_lo + 1, :], (8, 128))
         hi = jnp.broadcast_to(pool[above, at_hi : at_hi + 1, :], (8, 128))
         return shift_down(mid, first, lo), mid, shift_up(mid, last, hi)
 
-    for face, (delta, cell, z_cell) in enumerate(((0, 7, 7), (2, 0, 0))):
-        for outer in range(10):
-            dy = 0 if outer == 0 else (2 if outer == 9 else 1)
-            y = 7 if outer == 0 else (0 if outer == 9 else outer - 1)
-            put(face, outer, [column(half, delta * 9 + dy * 3, cell, y) for half in range(2)])
-        for x in range(8):
-            put(2 + face, x + 1, [column(half, 9 + delta * 3, x, cell) for half in range(2)])
-        for x in range(8):
-            parts = []
-            for half in range(2):
-                entry = entries[half][12 + delta]
-                if x in (0, 7):
-                    mid = pool[entry, pl.ds(ring_row(x, 0) + z_cell, 8, stride=8), :]
-                else:
-                    start = cell_row(x, 1, z_cell) - 1
-                    at_lo, at_hi = cell_row(x, 0, z_cell), cell_row(x, 7, z_cell)
-                    mid = pool[entry, start : start + 8, :]
-                    mid = jnp.where(first, jnp.broadcast_to(pool[entry, at_lo : at_lo + 1, :], (8, 128)), mid)
-                    mid = jnp.where(last, jnp.broadcast_to(pool[entry, at_hi : at_hi + 1, :], (8, 128)), mid)
-                parts.append((shift_down(mid, first, 0.0), mid, shift_up(mid, last, 0.0)))
-            put(4 + face, x + 1, parts)
+    def z_plane(here, x):
+        if x in (0, 7):
+            mid = pool[here, pl.ds(ring_row(x, 0) + z_cell, 8, stride=8), :]
+        else:
+            start = cell_row(x, 1, z_cell) - 1
+            at_lo, at_hi = cell_row(x, 0, z_cell), cell_row(x, 7, z_cell)
+            mid = pool[here, start : start + 8, :]
+            mid = jnp.where(first, jnp.broadcast_to(pool[here, at_lo : at_lo + 1, :], (8, 128)), mid)
+            mid = jnp.where(last, jnp.broadcast_to(pool[here, at_hi : at_hi + 1, :], (8, 128)), mid)
+        return shift_down(mid, first, 0.0), mid, shift_up(mid, last, 0.0)
+
+    for pair in range(BR // 2):
+        bricks = (2 * pair, 2 * pair + 1)
+        if face < 2:
+            around = [[[entry(b, delta * 9 + dy * 3 + dz) for dz in range(3)] for dy in range(3)] for b in bricks]
+            for outer in range(10):
+                dy = 0 if outer == 0 else (2 if outer == 9 else 1)
+                y = 7 if outer == 0 else (0 if outer == 9 else outer - 1)
+                put(pair, outer, [column(around[half][dy], cell, y) for half in range(2)])
+        elif face < 4:
+            around = [[entry(b, 9 + delta * 3 + dz) for dz in range(3)] for b in bricks]
+            for x in range(8):
+                put(pair, x + 1, [column(around[half], x, cell) for half in range(2)])
+        else:
+            here = [entry(b, 12 + delta) for b in bricks]
+            for x in range(8):
+                put(pair, x + 1, [z_plane(here[half], x) for half in range(2)])
 
 
 def halo_weights(w_ref, along):
@@ -248,23 +268,18 @@
             toeplitz(along.at[4 + face, shift], [w_ref[tap * 9 + shift * 3 + end] for tap in range(3)])
 
 
-def halo_sums(halo, along, sums):
+def sum_face(face, halo, along, sums):
     rows = 8 * BR
-    for face in range(6):
-        acc = jnp.zeros((4 * rows, 256), jnp.float32)
-        for shift in range(3):
-            for side in range(2):
-                part = halo[face, shift, side : side + 4].reshape(4 * rows, 256)
-                acc = acc + jnp.dot(part, along[face, shift, side], preferred_element_type=jnp.float32)
-        sums[face] = acc.reshape(4, BR, 8, 256)
+    acc = jnp.zeros((4 * rows, 256), jnp.float32)
+    for shift in range(3):
+        for side in range(2):
+            part = halo[face, shift, side : side + 4].reshape(4 * rows, 256)
+            acc = acc + jnp.dot(part, along[face, shift, side], preferred_element_type=jnp.float32)
+    sums[face] = acc.reshape(4, BR, 8, 256)
 
 
 def halo_part(src_ref, sources, landed, sems, streams, stream_sems, pool, halo, along, sums):
     loads = start_all([pltpu.make_async_copy(a, b, sems.at[n]) for n, (a, b) in enumerate(zip(sources, landed))])
-    for n, (source, target, size) in enumerate(streams):
-        for pair in range(BR // 2):
-            at = pl.ds(pair * size, size)
-            pltpu.make_async_copy(source.at[at], target.at[at], stream_sems.at[n, pair]).start()
     pool[BLANK] = jnp.zeros((SHELL, 128), jnp.float32)
     for face in range(2, 6):
         for shift in range(3):
@@ -274,14 +289,22 @@
     halo_weights(landed[0], along)
     for load, start, field in zip(loads[1:], (0, BR, BR + EDGE, BR + 2 * EDGE), landed[1:]):
         load.wait()
+        if field is landed[-1]:
+            start_streams(streams, stream_sems)
         fill_pool(pool, start, field)
 
-    def pair_body(pair, carry):
-        build_halos(pair, src_ref, pool, halo)
-        return carry
-
-    lax.fori_loop(0, BR // 2, pair_body, 0)
-    halo_sums(halo, along, sums)
+    build_face(0, src_ref, pool, halo)
+    for face in range(6):
+        if face < 5:
+            build_face(face + 1, src_ref, pool, halo)
+        sum_face(face, halo, along, sums)
+
+
+def start_streams(streams, stream_sems):
+    for pair in range(BR // 2):
+        for n, (source, target, size) in enumerate(streams):
+            at = pl.ds(pair * size, size)
+            pltpu.make_async_copy(source.at[at], target.at[at], stream_sems.at[n, pair]).start()
 
 
 def wait_stream(streams, stream_sems, pair):
@@ -327,17 +350,23 @@
         wait_stream(streams, stream_sems, pair)
         for half in range(2):
             brick = pair * 2 + half
+            planes = []
             for x in range(8):
                 rows = slice(x * 64, x * 64 + 64)
                 value = whole_plane(part, sums, pair, half, x)
                 value = value / (1.0 + jnp.exp(-value)) * mask[brick, rows, :].astype(jnp.float32)
                 done[brick, rows, :] = value.astype(jnp.bfloat16)
-            shell = jnp.dot(pick_ref[...], done[brick], preferred_element_type=jnp.float32)
-            own[brick] = shell.astype(jnp.bfloat16)
+                planes.append(value)
+            store_shell(own.at[brick], planes)
         store(pair).start()
         return carry
 
     lax.fori_loop(0, BR // 2, pair_body, 0)
+    for brick in range(0, BR, 2):
+        both = jnp.concatenate([done[brick], done[brick + 1]], axis=1)
+        inner = jnp.dot(pick_ref[...], both, preferred_element_type=jnp.float32).astype(jnp.bfloat16)
+        own[brick, FACE_LO:SHELL, :] = inner[:, :128]
+        own[brick + 1, FACE_LO:SHELL, :] = inner[:, 128:]
     copies = hand_out(send_ref, own, out_ref, low_ref, high_ref, out_sems)
     wait_all([store(pair) for pair in range(BR // 2)])
     wait_all(copies)
@@ -396,8 +425,8 @@
     return [jax.ShapeDtypeStruct((n, SHELL, 128), jnp.bfloat16) for n in counts]
 
 
-def params(mib):
-    return pltpu.CompilerParams(vmem_limit_bytes=mib * MIB)
+def params():
+    return pltpu.CompilerParams(vmem_limit_bytes=VMEM_LIMIT)
 
 
 def own_scratch():
@@ -433,16 +462,17 @@
 def pack(send, feats, occ, pick):
     return pl.pallas_call(
         pack_kernel,
-        in_specs=[SCALARS(), ANYWHERE(), WHOLE(), WHOLE()],
+        in_specs=[SCALARS(), ANYWHERE(), WHOLE(), ANYWHERE()],
         out_specs=[ANYWHERE()] * 3,
         out_shape=shells_of(SLOTS, EDGE, EDGE),
         scratch_shapes=[
             pltpu.VMEM((BR, 512, 128), jnp.bfloat16),
             pltpu.VMEM((BR, SHELL, 128), jnp.bfloat16),
-            pltpu.SemaphoreType.DMA((BR // 2,)),
+            pltpu.VMEM((SHELL, 512), jnp.bfloat16),
+            pltpu.SemaphoreType.DMA((BR // 2 + 1,)),
             pltpu.SemaphoreType.DMA((SLOTS + 2,)),
         ],
-        compiler_params=params(LIMIT),
+        compiler_params=params(),
         name="pack_shells",
     )(send, feats, occ, pick)
 
@@ -455,7 +485,7 @@
         out_specs=[part_spec(), pair_spec(), pair_spec(), shell_pair_spec()],
         out_shape=[PARTIAL, FIELD, FIELD] + shells_of(BR),
         scratch_shapes=own_scratch(),
-        compiler_params=params(LIMIT),
+        compiler_params=params(),
         cost_estimate=OWN_COST,
         name="first_own",
     )(feats, occ, pick, weights)
@@ -469,7 +499,7 @@
         out_specs=[part_spec(), shell_pair_spec()],
         out_shape=[PARTIAL] + shells_of(BR),
         scratch_shapes=own_scratch(),
-        compiler_params=params(LIMIT),
+        compiler_params=params(),
         cost_estimate=OWN_COST,
         name="second_own",
     )(hidden, x, pick, weights)
@@ -482,7 +512,7 @@
         out_specs=[ANYWHERE()] * 4,
         out_shape=[FIELD] + shells_of(SLOTS, EDGE, EDGE),
         scratch_shapes=halo_scratch() + own_shells_scratch(),
-        compiler_params=params(LIMIT),
+        compiler_params=params(),
         cost_estimate=HALO_COST,
         name="first_halo",
     )(src, send, pick, part, mask, weights, shells, before, after, recv)
@@ -495,7 +525,7 @@
         out_specs=ANYWHERE(),
         out_shape=FIELD,
         scratch_shapes=halo_scratch(),
-        compiler_params=params(LIMIT),
+        compiler_params=params(),
         cost_estimate=HALO_COST,
         name="second_halo",
     )(src, part, mask, weights, shells, before, after, recv)
@@ -518,6 +548,7 @@
     send = send_list.reshape(SLOTS)
     pick = shell_matrix()
     outgoing, low, high = pack(send, features, occupancy, pick)
+    pick = pick[FACE_LO:]
     around = exchange(outgoing, low, high)
     part, x, mask, shells = first_own(features, occupancy, pick, w_first)
     hidden, outgoing, low, high = first_halo(src_ref, send, pick, part, mask, w_first, shells, *around)

time: 91 us -> 83.9 us (0.922)
  Pallas kernels: 54.6 us -> 49.3 us
  local copies, waits for them, and re-layouts: 2.33 us -> 0 us
    pallas_call x1, Pallas kernels: 12 us -> 9.39 us  [first_halo(): pl.pallas_call(first_halo_kernel, in_specs=[SCALARS(), SCALARS(), WHOLE()...]
    unnamed x20 -> x0, local copies, waits for them, and re-layouts: 2.33 us -> none
  transfers between devices with their start and end apart: 6 -> 6, of which waited for: 0 -> 0; matrix products, arithmetic and copies ran while one was open for 0% -> 0% of each run, Pallas kernels for 31% -> 32%
where the time goes in v1:
time: 83.9 us; the launch traced here: 83.3 us
  Pallas kernels  49.3 us (59%)
  starting transfers between devices  33.7 us (40%)
    ppermute x4, starting transfers between devices, shifted(): lax.ppermute(value, axis, [(source, source + steps) for source in range(i...  22.2 us
    pallas_call x1, Pallas kernels, first_own(): pl.pallas_call(first_own_kernel, grid=GRID, in_specs=[pair_spec(), WHOLE(...  14.7 us
    pallas_call x1, Pallas kernels, second_own(): pl.pallas_call(second_own_kernel, grid=GRID, in_specs=[pair_spec(), pair_...  12.3 us
    all_to_all x2, starting transfers between devices, exchange(): lax.all_to_all(outgoing, 'dev', split_axis=0, concat_axis=0, tiled=True)  11.5 us
    pallas_call x1, Pallas kernels, first_halo(): pl.pallas_call(first_halo_kernel, in_specs=[SCALARS(), SCALARS(), WHOLE()...  9.39 us
    pallas_call x1, Pallas kernels, second_halo(): pl.pallas_call(second_halo_kernel, in_specs=[SCALARS()] + [ANYWHERE()] *...  8.27 us
    pallas_call x1, Pallas kernels, pack(): pl.pallas_call(pack_kernel, in_specs=[SCALARS(), ANYWHERE(), WHOLE(), ANY...  4.7 us
  transfers between devices with their start and end apart: 6, of which 0 were waited for; matrix products, arithmetic and copies ran while one was open for 0% of the time, Pallas kernels for 32%

profile of v1, /device:TPU:128, one launch (start us, length us, event | category | flops | bytes accessed | tf_op | source)
XLA Modules:
  0.0 83.3 jit_solution(3024581192073876325)
XLA Ops:
  0.0 4.7 %pack_shells.1 = (bf16[16,304,128]{2,1,0:T(8,128)(2,1)}, bf16[2,304,128]{2,1,0:T(8,128)(2,1)}, bf16[2,304,128]{2,1,0:T(8,128)(2,1)}) custom-call(s32[16]{0:T(128)} %bitcast.1, bf16[12,512,128]{2,1,0:T(8,128)(2,1)} %feat_ref.3, s32[12,512]{1,0:T(8,128)} %occ_ref.3, bf16[304,512]{1,0:T(8,128)(2,1)} %constant.2.clone.pick_ref), custom_call_target="tpu_custom_call" | custom-call | tf_op jit(solution)/shard_map/pack_shells/pallas_call | solution.py:463
  4.7 7.1 %all-to-all-start = ((bf16[16,304,128]{2,1,0:T(8,128)(2,1)}), bf16[16,304,128]{2,1,0:T(8,128)(2,1)}, u32[]{:S(2)}, u32[]{:S(2)}) async-start(bf16[16,304,128]{2,1,0:T(8,128)(2,1)} %get-tuple-element.23), calls=%async_computation | async-start | bytes 2490368 | tf_op jit(solution)/shard_map/all_to_all | solution.py:541
  11.8 3.8 %collective-permute-start = (bf16[2,304,128]{2,1,0:T(8,128)(2,1)}, bf16[2,304,128]{2,1,0:T(8,128)(2,1)}, u32[]{:S(2)}, u32[]{:S(2)}) collective-permute-start(bf16[2,304,128]{2,1,0:T(8,128)(2,1)} %get-tuple-element.21), channel_id=1, source_target_pairs={{0,1},{1,2},{2,3},{3,4},{4,5},{5,6},{6,7},{7,8},{8,9},{9,10},{10,1... | collective-permute-start | bytes 466952 | tf_op jit(solution)/shard_map/ppermute | solution.py:537
  15.6 7.2 %collective-permute-start.1 = (bf16[2,304,128]{2,1,0:T(8,128)(2,1)}, bf16[2,304,128]{2,1,0:T(8,128)(2,1)}, u32[]{:S(2)}, u32[]{:S(2)}) collective-permute-start(bf16[2,304,128]{2,1,0:T(8,128)(2,1)} %get-tuple-element.22), channel_id=1, source_target_pairs={{1,0},{2,1},{3,2},{4,3},{5,4},{6,5},{7,6},{8,7},{9,8},{10,9},{11,1... | collective-permute-start | bytes 466952 | tf_op jit(solution)/shard_map/ppermute | solution.py:537
  22.8 14.7 %first_own.1 = (f32[6,512,256]{2,1,0:T(8,128)}, bf16[12,512,128]{2,1,0:T(8,128)(2,1)}, bf16[12,512,128]{2,1,0:T(8,128)(2,1)}, bf16[12,304,128]{2,1,0:T(8,128)(2,1)}) custom-call(bf16[12,512,128]{2,1,0:T(8,128)(2,1)} %feat_ref.3, s32[12,512]{1,0:T(8,128)} %occ_ref.3, bf16[80,512]{1,0:T(8,128)(2,1)} %constant.7.pick_ref, bf16[27,128,128]{2,1,0:T(8,128)(2,1)} %w_ref.5), custom_call_target="tpu_custom_call" | custom-call | flops 7247757312 | bytes 8388608 | tf_op jit(solution)/shard_map/first_own/pallas_call | solution.py:481
  37.5 0.0 collective-permute-done.before_ref
  37.5 0.0 collective-permute-done.1.after_ref
  37.5 0.0 all-to-all-done.recv_ref
  37.5 9.4 %first_halo.1 = (bf16[12,512,128]{2,1,0:T(8,128)(2,1)}, bf16[16,304,128]{2,1,0:T(8,128)(2,1)}, bf16[2,304,128]{2,1,0:T(8,128)(2,1)}, bf16[2,304,128]{2,1,0:T(8,128)(2,1)}) custom-call(s32[12,27]{1,0:T(8,128)} %src_ref.3, s32[16]{0:T(128)} %bitcast.2, bf16[80,512]{1,0:T(8,128)(2,1)} %constant.7.pick_ref, f32[6,512,256]{2,1,0:T(8,128)} %get-tuple-element.18.part_ref, ...), custom_call_target="tpu_custom_call" | custom-call | flops 1811939328 | bytes 10485760 | tf_op jit(solution)/shard_map/first_halo/pallas_call | solution.py:509
  46.9 4.4 %all-to-all-start.1 = ((bf16[16,304,128]{2,1,0:T(8,128)(2,1)}), bf16[16,304,128]{2,1,0:T(8,128)(2,1)}, u32[]{:S(2)}, u32[]{:S(2)}) async-start(bf16[16,304,128]{2,1,0:T(8,128)(2,1)} %get-tuple-element.30), calls=%async_computation.1 | async-start | bytes 2490368 | tf_op jit(solution)/shard_map/all_to_all | solution.py:541
  51.3 3.6 %collective-permute-start.2 = (bf16[2,304,128]{2,1,0:T(8,128)(2,1)}, bf16[2,304,128]{2,1,0:T(8,128)(2,1)}, u32[]{:S(2)}, u32[]{:S(2)}) collective-permute-start(bf16[2,304,128]{2,1,0:T(8,128)(2,1)} %get-tuple-element.28), channel_id=1, source_target_pairs={{0,1},{1,2},{2,3},{3,4},{4,5},{5,6},{6,7},{7,8},{8,9},{9,10},{10,1... | collective-permute-start | bytes 466952 | tf_op jit(solution)/shard_map/ppermute | solution.py:537
  55.0 7.5 %collective-permute-start.3 = (bf16[2,304,128]{2,1,0:T(8,128)(2,1)}, bf16[2,304,128]{2,1,0:T(8,128)(2,1)}, u32[]{:S(2)}, u32[]{:S(2)}) collective-permute-start(bf16[2,304,128]{2,1,0:T(8,128)(2,1)} %get-tuple-element.29), channel_id=1, source_target_pairs={{1,0},{2,1},{3,2},{4,3},{5,4},{6,5},{7,6},{8,7},{9,8},{10,9},{11,1... | collective-permute-start | bytes 466952 | tf_op jit(solution)/shard_map/ppermute | solution.py:537
  62.5 12.3 %second_own.1 = (f32[6,512,256]{2,1,0:T(8,128)}, bf16[12,304,128]{2,1,0:T(8,128)(2,1)}) custom-call(bf16[12,512,128]{2,1,0:T(8,128)(2,1)} %get-tuple-element.24.hidden_ref, bf16[12,512,128]{2,1,0:T(8,128)(2,1)} %get-tuple-element.25.x_ref, bf16[80,512]{1,0:T(8,128)(2,1)} %constant.7.pick_ref, bf16[27,128,128]{2,1,0:T(8,128)(2,1)} %w_ref.7), custom_call_target="tpu_custom_call" | custom-call | flops 7247757312 | bytes 8388608 | tf_op jit(solution)/shard_map/second_own/pallas_call | solution.py:495
  74.8 0.0 collective-permute-done.2.before_ref
  74.8 0.0 collective-permute-done.3.after_ref
  74.8 0.0 all-to-all-done.1.recv_ref
  74.8 8.3 %second_halo.1 = bf16[12,512,128]{2,1,0:T(8,128)(2,1)} custom-call(s32[12,27]{1,0:T(8,128)} %src_ref.3, f32[6,512,256]{2,1,0:T(8,128)} %get-tuple-element.26.part_ref, bf16[12,512,128]{2,1,0:T(8,128)(2,1)} %get-tuple-element.19.mask_ref, bf16[27,128,128]{2,1,0:T(8,128)(2,1)} %w_ref.7, bf16[12,304,128]{2,1,0:T(8,128)(2,1)} %get-tuple-element.27.shells_ref, ...), custom_call_target="tpu_custom_call" | custom-call | flops 1811939328 | bytes 10485760 | tf_op jit(solution)/shard_map/second_halo/pallas_call | solution.py:522
Async XLA Ops:
  4.7 32.8 %all-to-all-start = ((bf16[16,304,128]{2,1,0:T(8,128)(2,1)}), bf16[16,304,128]{2,1,0:T(8,128)(2,1)}, u32[]{:S(2)}, u32[]{:S(2)}) async-start(bf16[16,304,128]{2,1,0:T(8,128)(2,1)} %get-tuple-element.23), calls=%async_computation | async-start | bytes 2490368 | tf_op jit(solution)/shard_map/all_to_all | solution.py:541
  11.8 25.7 %collective-permute-start = (bf16[2,304,128]{2,1,0:T(8,128)(2,1)}, bf16[2,304,128]{2,1,0:T(8,128)(2,1)}, u32[]{:S(2)}, u32[]{:S(2)}) collective-permute-start(bf16[2,304,128]{2,1,0:T(8,128)(2,1)} %get-tuple-element.21), channel_id=1, source_target_pairs={{0,1},{1,2},{2,3},{3,4},{4,5},{5,6},{6,7},{7,8},{8,9},{9,10},{10,1... | collective-permute-start | bytes 466952 | tf_op jit(solution)/shard_map/ppermute | solution.py:537
  15.6 21.9 %collective-permute-start.1 = (bf16[2,304,128]{2,1,0:T(8,128)(2,1)}, bf16[2,304,128]{2,1,0:T(8,128)(2,1)}, u32[]{:S(2)}, u32[]{:S(2)}) collective-permute-start(bf16[2,304,128]{2,1,0:T(8,128)(2,1)} %get-tuple-element.22), channel_id=1, source_target_pairs={{1,0},{2,1},{3,2},{4,3},{5,4},{6,5},{7,6},{8,7},{9,8},{10,9},{11,1... | collective-permute-start | bytes 466952 | tf_op jit(solution)/shard_map/ppermute | solution.py:537
  46.9 27.9 %all-to-all-start.1 = ((bf16[16,304,128]{2,1,0:T(8,128)(2,1)}), bf16[16,304,128]{2,1,0:T(8,128)(2,1)}, u32[]{:S(2)}, u32[]{:S(2)}) async-start(bf16[16,304,128]{2,1,0:T(8,128)(2,1)} %get-tuple-element.30), calls=%async_computation.1 | async-start | bytes 2490368 | tf_op jit(solution)/shard_map/all_to_all | solution.py:541
  51.3 23.5 %collective-permute-start.2 = (bf16[2,304,128]{2,1,0:T(8,128)(2,1)}, bf16[2,304,128]{2,1,0:T(8,128)(2,1)}, u32[]{:S(2)}, u32[]{:S(2)}) collective-permute-start(bf16[2,304,128]{2,1,0:T(8,128)(2,1)} %get-tuple-element.28), channel_id=1, source_target_pairs={{0,1},{1,2},{2,3},{3,4},{4,5},{5,6},{6,7},{7,8},{8,9},{9,10},{10,1... | collective-permute-start | bytes 466952 | tf_op jit(solution)/shard_map/ppermute | solution.py:537
  55.0 19.8 %collective-permute-start.3 = (bf16[2,304,128]{2,1,0:T(8,128)(2,1)}, bf16[2,304,128]{2,1,0:T(8,128)(2,1)}, u32[]{:S(2)}, u32[]{:S(2)}) collective-permute-start(bf16[2,304,128]{2,1,0:T(8,128)(2,1)} %get-tuple-element.29), channel_id=1, source_target_pairs={{1,0},{2,1},{3,2},{4,3},{5,4},{6,5},{7,6},{8,7},{9,8},{10,9},{11,1... | collective-permute-start | bytes 466952 | tf_op jit(solution)/shard_map/ppermute | solution.py:537

commit v2 on v1

--- a/solution.py
+++ b/solution.py
@@ -53,16 +53,27 @@
     return jnp.asarray(picked, jnp.bfloat16)
 
 
-def store_shell(shell, planes, cells=None, pick=None):
+def store_shell(shell, planes):
     shell[0:64, :] = planes[0].astype(jnp.bfloat16)
     shell[64:128, :] = planes[7].astype(jnp.bfloat16)
     for x in (1, 3, 5):
         for start, rows in ((128, slice(0, 8)), (176, slice(56, 64))):
             both = jnp.concatenate([planes[x][rows], planes[x + 1][rows]], axis=0)
             shell[start + (x - 1) * 8 : start + (x + 1) * 8, :] = both.astype(jnp.bfloat16)
-    if cells is not None:
-        inner = jnp.dot(pick, cells, preferred_element_type=jnp.float32)
-        shell[FACE_LO:SHELL, :] = inner.astype(jnp.bfloat16)
+
+
+def store_inner(shell, planes, cells, inner):
+    for x in range(1, 7):
+        rows = (x - 1) * 6
+        cells[x * 64 : x * 64 + 64, :] = planes[x]
+        inner[rows : rows + 6, :] = cells[pl.ds(x * 64 + 8, 6, stride=8), :]
+        inner[rows + 36 : rows + 42, :] = cells[pl.ds(x * 64 + 15, 6, stride=8), :]
+    inner[72:80, :] = jnp.zeros((8, 128), jnp.float32)
+    shell[FACE_LO:SHELL, :] = inner[...].astype(jnp.bfloat16)
+
+
+def parity():
+    return lax.rem(lax.axis_index("dev"), 2)
 
 
 def start_all(copies):
@@ -76,9 +87,10 @@
         copy.wait()
 
 
-def hand_out(send_ref, own, out_ref, low_ref, high_ref, sems):
-    copies = [pltpu.make_async_copy(own.at[:EDGE], high_ref, sems.at[SLOTS])]
-    copies.append(pltpu.make_async_copy(own.at[BR - EDGE :], low_ref, sems.at[SLOTS + 1]))
+def hand_out(send_ref, odd, own, out_ref, near_ref, far_ref, sems):
+    first, second = jnp.where(odd == 0, BR - EDGE, 0), jnp.where(odd == 0, 0, BR - EDGE)
+    copies = [pltpu.make_async_copy(own.at[pl.ds(first, EDGE)], near_ref, sems.at[SLOTS])]
+    copies.append(pltpu.make_async_copy(own.at[pl.ds(second, EDGE)], far_ref, sems.at[SLOTS + 1]))
     for slot in range(SLOTS):
         brick = jnp.maximum(send_ref[slot], 0)
         copies.append(pltpu.make_async_copy(own.at[brick], out_ref.at[slot], sems.at[slot]))
@@ -86,7 +98,7 @@
 
 
 def pack_kernel(
-    send_ref, feat_ref, occ_ref, pick_ref, out_ref, low_ref, high_ref, feats, own, pick, in_sems, out_sems
+    send_ref, feat_ref, occ_ref, pick_ref, out_ref, near_ref, far_ref, feats, own, pick, in_sems, out_sems
 ):
     pick_load = pltpu.make_async_copy(pick_ref, pick, in_sems.at[BR // 2])
     pick_load.start()
@@ -102,7 +114,7 @@
             chooser = pick[...] * jnp.broadcast_to(held, (SHELL, 512))
             shell = jnp.dot(chooser, feats[brick], preferred_element_type=jnp.float32)
             own[brick] = shell.astype(jnp.bfloat16)
-    wait_all(hand_out(send_ref, own, out_ref, low_ref, high_ref, out_sems))
+    wait_all(hand_out(send_ref, parity(), own, out_ref, near_ref, far_ref, out_sems))
 
 
 def toeplitz(target, taps):
@@ -173,7 +185,7 @@
                 part_ref[0, row : row + 8, lanes] = acc[row : row + 8, lanes] + added[y * 8 : y * 8 + 8]
 
 
-def first_own_kernel(feat_ref, occ_ref, pick_ref, w_ref, part_ref, x_ref, mask_ref, shell_ref, wide, block):
+def first_own_kernel(feat_ref, occ_ref, w_ref, part_ref, x_ref, mask_ref, shell_ref, wide, block, cells, inner):
     step = pl.program_id(0)
     rows = lax.broadcasted_iota(jnp.int32, (128, 128), 0)
     cols = lax.broadcasted_iota(jnp.int32, (128, 128), 1)
@@ -183,23 +195,26 @@
     for half in range(2):
         occupied = occ_ref[pl.ds(step * 2 + half, 1), :].astype(jnp.float32)
         for chunk in range(4):
-            cells = slice(chunk * 128, chunk * 128 + 128)
-            scale = jnp.where(diagonal, jnp.broadcast_to(occupied[:, cells], (128, 128)), 0.0).astype(jnp.bfloat16)
-            right = jnp.concatenate([feat_ref[half, cells, :], ones], axis=1)
+            at = slice(chunk * 128, chunk * 128 + 128)
+            scale = jnp.where(diagonal, jnp.broadcast_to(occupied[:, at], (128, 128)), 0.0).astype(jnp.bfloat16)
+            right = jnp.concatenate([feat_ref[half, at, :], ones], axis=1)
             both = jnp.dot(scale, right, preferred_element_type=jnp.float32)
-            x_ref[half, cells, :] = both[:, :128].astype(jnp.bfloat16)
-            mask_ref[half, cells, :] = both[:, 128:].astype(jnp.bfloat16)
+            x_ref[half, at, :] = both[:, :128].astype(jnp.bfloat16)
+            mask_ref[half, at, :] = both[:, 128:].astype(jnp.bfloat16)
             held[half, 2 * chunk] = both[:64, :128]
             held[half, 2 * chunk + 1] = both[64:, :128]
-        store_shell(shell_ref.at[half], [held[half, x] for x in range(8)], x_ref[half], pick_ref[...])
+        planes = [held[half, x] for x in range(8)]
+        store_shell(shell_ref.at[half], planes)
+        store_inner(shell_ref.at[half], planes, cells.at[half], inner.at[half])
     own_conv(lambda half, x: held[half, x], w_ref, part_ref, wide, block)
 
 
-def second_own_kernel(hidden_ref, x_ref, pick_ref, w_ref, part_ref, shell_ref, wide, block):
+def second_own_kernel(hidden_ref, x_ref, w_ref, part_ref, shell_ref, wide, block, cells, inner):
     plane = lambda ref: lambda half, x: ref[half, x * 64 : x * 64 + 64, :].astype(jnp.float32)
     for half in range(2):
         planes = [plane(hidden_ref)(half, x) for x in range(8)]
-        store_shell(shell_ref.at[half], planes, hidden_ref[half], pick_ref[...])
+        store_shell(shell_ref.at[half], planes)
+        store_inner(shell_ref.at[half], planes, cells.at[half], inner.at[half])
     own_conv(plane(hidden_ref), w_ref, part_ref, wide, block, plane(x_ref))
 
 
@@ -278,16 +293,17 @@
     sums[face] = acc.reshape(4, BR, 8, 256)
 
 
-def halo_part(src_ref, sources, landed, sems, streams, stream_sems, pool, halo, along, sums):
+def halo_part(odd, src_ref, sources, landed, sems, streams, stream_sems, pool, halo, along, sums):
     loads = start_all([pltpu.make_async_copy(a, b, sems.at[n]) for n, (a, b) in enumerate(zip(sources, landed))])
     pool[BLANK] = jnp.zeros((SHELL, 128), jnp.float32)
     for face in range(2, 6):
         for shift in range(3):
             halo[face, shift, 0, :, 0:128] = jnp.zeros((8 * BR, 128), jnp.bfloat16)
             halo[face, shift, 4, :, 128:256] = jnp.zeros((8 * BR, 128), jnp.bfloat16)
+    near, far = BR + EDGE * (1 - odd), BR + EDGE * odd
     loads[0].wait()
     halo_weights(landed[0], along)
-    for load, start, field in zip(loads[1:], (0, BR, BR + EDGE, BR + 2 * EDGE), landed[1:]):
+    for load, start, field in zip(loads[1:], (0, near, far, BR + 2 * EDGE), landed[1:]):
         load.wait()
         if field is landed[-1]:
             start_streams(streams, stream_sems)
@@ -332,15 +348,15 @@
 
 
 def first_halo_kernel(
-    src_ref, send_ref, pick_ref, part_ref, mask_ref, w_ref, shells_ref, before_ref, after_ref, recv_ref,
-    hidden_ref, out_ref, low_ref, high_ref,
-    pool, halo, along, sums, w, shells, before, after, recv, part, mask, done, sems, stream_sems, done_sems,
+    src_ref, send_ref, pick_ref, part_ref, mask_ref, w_ref, shells_ref, near_in_ref, far_in_ref, recv_ref,
+    hidden_ref, out_ref, near_ref, far_ref,
+    pool, halo, along, sums, w, shells, near, far, recv, part, mask, done, sems, stream_sems, done_sems,
     own, out_sems,
 ):
     streams = ((part_ref, part, 1), (mask_ref, mask, 2))
-    sources = (w_ref, shells_ref, before_ref, after_ref, recv_ref)
-    landed = (w, shells, before, after, recv)
-    halo_part(src_ref, sources, landed, sems, streams, stream_sems, pool, halo, along, sums)
+    sources = (w_ref, shells_ref, near_in_ref, far_in_ref, recv_ref)
+    landed = (w, shells, near, far, recv)
+    halo_part(parity(), src_ref, sources, landed, sems, streams, stream_sems, pool, halo, along, sums)
 
     def store(pair):
         at = pl.ds(pair * 2, 2)
@@ -367,20 +383,20 @@
         inner = jnp.dot(pick_ref[...], both, preferred_element_type=jnp.float32).astype(jnp.bfloat16)
         own[brick, FACE_LO:SHELL, :] = inner[:, :128]
         own[brick + 1, FACE_LO:SHELL, :] = inner[:, 128:]
-    copies = hand_out(send_ref, own, out_ref, low_ref, high_ref, out_sems)
+    copies = hand_out(send_ref, parity(), own, out_ref, near_ref, far_ref, out_sems)
     wait_all([store(pair) for pair in range(BR // 2)])
     wait_all(copies)
 
 
 def second_halo_kernel(
-    src_ref, part_ref, mask_ref, w_ref, shells_ref, before_ref, after_ref, recv_ref,
+    src_ref, part_ref, mask_ref, w_ref, shells_ref, near_in_ref, far_in_ref, recv_ref,
     result_ref,
-    pool, halo, along, sums, w, shells, before, after, recv, part, mask, done, sems, stream_sems, done_sems,
+    pool, halo, along, sums, w, shells, near, far, recv, part, mask, done, sems, stream_sems, done_sems,
 ):
     streams = ((part_ref, part, 1), (mask_ref, mask, 2))
-    sources = (w_ref, shells_ref, before_ref, after_ref, recv_ref)
-    landed = (w, shells, before, after, recv)
-    halo_part(src_ref, sources, landed, sems, streams, stream_sems, pool, halo, along, sums)
+    sources = (w_ref, shells_ref, near_in_ref, far_in_ref, recv_ref)
+    landed = (w, shells, near, far, recv)
+    halo_part(parity(), src_ref, sources, landed, sems, streams, stream_sems, pool, halo, along, sums)
 
     def store(pair):
         at = pl.ds(pair * 2, 2)
@@ -430,7 +446,12 @@
 
 
 def own_scratch():
-    return [pltpu.VMEM((9, 2, 256, 256), jnp.bfloat16), pltpu.VMEM((3, 5, 10, 16, 256), jnp.bfloat16)]
+    return [
+        pltpu.VMEM((9, 2, 256, 256), jnp.bfloat16),
+        pltpu.VMEM((3, 5, 10, 16, 256), jnp.bfloat16),
+        pltpu.VMEM((2, 512, 128), jnp.float32),
+        pltpu.VMEM((2, SHELL - FACE_LO, 128), jnp.float32),
+    ]
 
 
 def halo_scratch():
@@ -477,35 +498,35 @@
     )(send, feats, occ, pick)
 
 
-def first_own(feats, occ, pick, weights):
+def first_own(feats, occ, weights):
     return pl.pallas_call(
         first_own_kernel,
         grid=GRID,
-        in_specs=[pair_spec(), WHOLE(), WHOLE(), WHOLE()],
+        in_specs=[pair_spec(), WHOLE(), WHOLE()],
         out_specs=[part_spec(), pair_spec(), pair_spec(), shell_pair_spec()],
         out_shape=[PARTIAL, FIELD, FIELD] + shells_of(BR),
         scratch_shapes=own_scratch(),
         compiler_params=params(),
         cost_estimate=OWN_COST,
         name="first_own",
-    )(feats, occ, pick, weights)
-
-
-def second_own(hidden, x, pick, weights):
+    )(feats, occ, weights)
+
+
+def second_own(hidden, x, weights):
     return pl.pallas_call(
         second_own_kernel,
         grid=GRID,
-        in_specs=[pair_spec(), pair_spec(), WHOLE(), WHOLE()],
+        in_specs=[pair_spec(), pair_spec(), WHOLE()],
         out_specs=[part_spec(), shell_pair_spec()],
         out_shape=[PARTIAL] + shells_of(BR),
         scratch_shapes=own_scratch(),
         compiler_params=params(),
         cost_estimate=OWN_COST,
         name="second_own",
-    )(hidden, x, pick, weights)
-
-
-def first_halo(src, send, pick, part, mask, weights, shells, before, after, recv):
+    )(hidden, x, weights)
+
+
+def first_halo(src, send, pick, part, mask, weights, shells, near, far, recv):
     return pl.pallas_call(
         first_halo_kernel,
         in_specs=[SCALARS(), SCALARS(), WHOLE()] + [ANYWHERE()] * 7,
@@ -515,10 +536,10 @@
         compiler_params=params(),
         cost_estimate=HALO_COST,
         name="first_halo",
-    )(src, send, pick, part, mask, weights, shells, before, after, recv)
-
-
-def second_halo(src, part, mask, weights, shells, before, after, recv):
+    )(src, send, pick, part, mask, weights, shells, near, far, recv)
+
+
+def second_halo(src, part, mask, weights, shells, near, far, recv):
     return pl.pallas_call(
         second_halo_kernel,
         in_specs=[SCALARS()] + [ANYWHERE()] * 7,
@@ -528,32 +549,32 @@
         compiler_params=params(),
         cost_estimate=HALO_COST,
         name="second_halo",
-    )(src, part, mask, weights, shells, before, after, recv)
-
-
-def shifted(value, axis, steps):
-    count = lax.axis_size(axis)
-    initial, last = (max(0, -steps), min(count, count - steps))
-    return lax.ppermute(value, axis, [(source, source + steps) for source in range(initial, last)])
-
-
-def exchange(outgoing, low, high):
+    )(src, part, mask, weights, shells, near, far, recv)
+
+
+def swapped(value, begin):
+    axes = ("grp", "dev")
+    routes = []
+    for device in range(begin, lax.axis_size(axes) - 1, 2):
+        routes += [(device, device + 1), (device + 1, device)]
+    return lax.ppermute(value, axes, routes)
+
+
+def exchange(outgoing, near, far):
     arrived = lax.all_to_all(outgoing, "dev", split_axis=0, concat_axis=0, tiled=True)
-    before = shifted(low, ("grp", "dev"), 1)
-    after = shifted(high, ("grp", "dev"), -1)
-    return before, after, arrived
+    return swapped(near, 0), swapped(far, 1), arrived
 
 
 def per_device(features, occupancy, w_first, w_second, src_ref, send_list):
     send = send_list.reshape(SLOTS)
     pick = shell_matrix()
-    outgoing, low, high = pack(send, features, occupancy, pick)
+    outgoing, near, far = pack(send, features, occupancy, pick)
     pick = pick[FACE_LO:]
-    around = exchange(outgoing, low, high)
-    part, x, mask, shells = first_own(features, occupancy, pick, w_first)
-    hidden, outgoing, low, high = first_halo(src_ref, send, pick, part, mask, w_first, shells, *around)
-    around = exchange(outgoing, low, high)
-    part, shells = second_own(hidden, x, pick, w_second)
+    around = exchange(outgoing, near, far)
+    part, x, mask, shells = first_own(features, occupancy, w_first)
+    hidden, outgoing, near, far = first_halo(src_ref, send, pick, part, mask, w_first, shells, *around)
+    around = exchange(outgoing, near, far)
+    part, shells = second_own(hidden, x, w_second)
     return second_halo(src_ref, part, mask, w_second, shells, *around)
 
 

time: 83.9 us -> 79.6 us (0.949)
  the two profiles are of different devices: /device:TPU:128 before, /device:TPU:65 now
where the time goes in v2:
time: 79.6 us; the launch traced here: 79.1 us
  Pallas kernels  46.9 us (59%)
  starting transfers between devices  28 us (35%)
  waiting for transfers between devices  4.05 us (5%)
    ppermute x4, starting transfers between devices, swapped(): return lax.ppermute(value, axes, routes)  16.7 us
    pallas_call x1, Pallas kernels, first_own(): pl.pallas_call(first_own_kernel, grid=GRID, in_specs=[pair_spec(), WHOLE(...  13 us
    pallas_call x1, Pallas kernels, second_own(): pl.pallas_call(second_own_kernel, grid=GRID, in_specs=[pair_spec(), pair_...  11.5 us
    all_to_all x2, starting transfers between devices, exchange(): lax.all_to_all(outgoing, 'dev', split_axis=0, concat_axis=0, tiled=True)  11.2 us
    pallas_call x1, Pallas kernels, first_halo(): pl.pallas_call(first_halo_kernel, in_specs=[SCALARS(), SCALARS(), WHOLE()...  9.42 us
    pallas_call x1, Pallas kernels, second_halo(): pl.pallas_call(second_halo_kernel, in_specs=[SCALARS()] + [ANYWHERE()] *...  8.27 us
    pallas_call x1, Pallas kernels, pack(): pl.pallas_call(pack_kernel, in_specs=[SCALARS(), ANYWHERE(), WHOLE(), ANY...  4.69 us
    ppermute x4, waiting for transfers between devices, swapped(): return lax.ppermute(value, axes, routes)  4.04 us
  transfers between devices with their start and end apart: 6, of which 2 were waited for; matrix products, arithmetic and copies ran while one was open for 0% of the time, Pallas kernels for 31%

profile of v2, /device:TPU:65, one launch (start us, length us, event | category | flops | bytes accessed | tf_op | source)
XLA Modules:
  0.0 79.1 jit_solution(15343250591742243387)
XLA Ops:
  0.0 4.7 %pack_shells.1 = (bf16[16,304,128]{2,1,0:T(8,128)(2,1)}, bf16[2,304,128]{2,1,0:T(8,128)(2,1)}, bf16[2,304,128]{2,1,0:T(8,128)(2,1)}) custom-call(s32[16]{0:T(128)} %bitcast.1, bf16[12,512,128]{2,1,0:T(8,128)(2,1)} %feat_ref.3, s32[12,512]{1,0:T(8,128)} %occ_ref.3, bf16[304,512]{1,0:T(8,128)(2,1)} %constant.2.clone.pick_ref), custom_call_target="tpu_custom_call" | custom-call | tf_op jit(solution)/shard_map/pack_shells/pallas_call | solution.py:484
  4.7 6.8 %all-to-all-start = ((bf16[16,304,128]{2,1,0:T(8,128)(2,1)}), bf16[16,304,128]{2,1,0:T(8,128)(2,1)}, u32[]{:S(2)}, u32[]{:S(2)}) async-start(bf16[16,304,128]{2,1,0:T(8,128)(2,1)} %get-tuple-element.23), calls=%async_computation | async-start | bytes 2490368 | tf_op jit(solution)/shard_map/all_to_all | solution.py:564
  11.5 1.3 %collective-permute-start = (bf16[2,304,128]{2,1,0:T(8,128)(2,1)}, bf16[2,304,128]{2,1,0:T(8,128)(2,1)}, u32[]{:S(2)}, u32[]{:S(2)}) collective-permute-start(bf16[2,304,128]{2,1,0:T(8,128)(2,1)} %get-tuple-element.21), channel_id=1, source_target_pairs={{0,1},{1,0},{2,3},{3,2},{4,5},{5,4},{6,7},{7,6},{8,9},{9,8},{10,11... | collective-permute-start | bytes 466952 | tf_op jit(solution)/shard_map/ppermute | solution.py:560
  12.8 7.2 %collective-permute-start.1 = (bf16[2,304,128]{2,1,0:T(8,128)(2,1)}, bf16[2,304,128]{2,1,0:T(8,128)(2,1)}, u32[]{:S(2)}, u32[]{:S(2)}) collective-permute-start(bf16[2,304,128]{2,1,0:T(8,128)(2,1)} %get-tuple-element.22), channel_id=1, source_target_pairs={{1,2},{2,1},{3,4},{4,3},{5,6},{6,5},{7,8},{8,7},{9,10},{10,9},{11,... | collective-permute-start | bytes 466952 | tf_op jit(solution)/shard_map/ppermute | solution.py:560
  20.0 13.0 %first_own.1 = (f32[6,512,256]{2,1,0:T(8,128)}, bf16[12,512,128]{2,1,0:T(8,128)(2,1)}, bf16[12,512,128]{2,1,0:T(8,128)(2,1)}, bf16[12,304,128]{2,1,0:T(8,128)(2,1)}) custom-call(bf16[12,512,128]{2,1,0:T(8,128)(2,1)} %feat_ref.3, s32[12,512]{1,0:T(8,128)} %occ_ref.3, bf16[27,128,128]{2,1,0:T(8,128)(2,1)} %w_ref.5), custom_call_target="tpu_custom_call" | custom-call | flops 7247757312 | bytes 8388608 | tf_op jit(solution)/shard_map/first_own/pallas_call | solution.py:502
  33.0 0.0 collective-permute-done.near_in_ref
  33.1 1.1 %collective-permute-done.1.far_in_ref = bf16[2,304,128]{2,1,0:T(8,128)(2,1)} collective-permute-done((bf16[2,304,128]{2,1,0:T(8,128)(2,1)}, bf16[2,304,128]{2,1,0:T(8,128)(2,1)}, u32[]{:S(2)}, u32[]{:S(2)}) %collective-permute-start.1) | collective-permute-done | bytes 155680 | tf_op jit(solution)/shard_map/ppermute | solution.py:560
  34.1 0.0 all-to-all-done.recv_ref
  34.1 9.4 %first_halo.1 = (bf16[12,512,128]{2,1,0:T(8,128)(2,1)}, bf16[16,304,128]{2,1,0:T(8,128)(2,1)}, bf16[2,304,128]{2,1,0:T(8,128)(2,1)}, bf16[2,304,128]{2,1,0:T(8,128)(2,1)}) custom-call(s32[12,27]{1,0:T(8,128)} %src_ref.3, s32[16]{0:T(128)} %bitcast.2, bf16[80,512]{1,0:T(8,128)(2,1)} %constant.7.pick_ref, f32[6,512,256]{2,1,0:T(8,128)} %get-tuple-element.18.part_ref, ...), custom_call_target="tpu_custom_call" | custom-call | flops 1811939328 | bytes 10485760 | tf_op jit(solution)/shard_map/first_halo/pallas_call | solution.py:530
  43.5 4.4 %all-to-all-start.1 = ((bf16[16,304,128]{2,1,0:T(8,128)(2,1)}), bf16[16,304,128]{2,1,0:T(8,128)(2,1)}, u32[]{:S(2)}, u32[]{:S(2)}) async-start(bf16[16,304,128]{2,1,0:T(8,128)(2,1)} %get-tuple-element.30), calls=%async_computation.1 | async-start | bytes 2490368 | tf_op jit(solution)/shard_map/all_to_all | solution.py:564
  47.9 1.2 %collective-permute-start.2 = (bf16[2,304,128]{2,1,0:T(8,128)(2,1)}, bf16[2,304,128]{2,1,0:T(8,128)(2,1)}, u32[]{:S(2)}, u32[]{:S(2)}) collective-permute-start(bf16[2,304,128]{2,1,0:T(8,128)(2,1)} %get-tuple-element.28), channel_id=1, source_target_pairs={{0,1},{1,0},{2,3},{3,2},{4,5},{5,4},{6,7},{7,6},{8,9},{9,8},{10,11... | collective-permute-start | bytes 466952 | tf_op jit(solution)/shard_map/ppermute | solution.py:560
  49.1 7.0 %collective-permute-start.3 = (bf16[2,304,128]{2,1,0:T(8,128)(2,1)}, bf16[2,304,128]{2,1,0:T(8,128)(2,1)}, u32[]{:S(2)}, u32[]{:S(2)}) collective-permute-start(bf16[2,304,128]{2,1,0:T(8,128)(2,1)} %get-tuple-element.29), channel_id=1, source_target_pairs={{1,2},{2,1},{3,4},{4,3},{5,6},{6,5},{7,8},{8,7},{9,10},{10,9},{11,... | collective-permute-start | bytes 466952 | tf_op jit(solution)/shard_map/ppermute | solution.py:560
  56.2 11.5 %second_own.1 = (f32[6,512,256]{2,1,0:T(8,128)}, bf16[12,304,128]{2,1,0:T(8,128)(2,1)}) custom-call(bf16[12,512,128]{2,1,0:T(8,128)(2,1)} %get-tuple-element.24.hidden_ref, bf16[12,512,128]{2,1,0:T(8,128)(2,1)} %get-tuple-element.25.x_ref, bf16[27,128,128]{2,1,0:T(8,128)(2,1)} %w_ref.7), custom_call_target="tpu_custom_call" | custom-call | flops 7247757312 | bytes 8388608 | tf_op jit(solution)/shard_map/second_own/pallas_call | solution.py:516
  67.6 0.0 collective-permute-done.2.near_in_ref
  67.6 3.0 %collective-permute-done.3.far_in_ref = bf16[2,304,128]{2,1,0:T(8,128)(2,1)} collective-permute-done((bf16[2,304,128]{2,1,0:T(8,128)(2,1)}, bf16[2,304,128]{2,1,0:T(8,128)(2,1)}, u32[]{:S(2)}, u32[]{:S(2)}) %collective-permute-start.3) | collective-permute-done | bytes 155680 | tf_op jit(solution)/shard_map/ppermute | solution.py:560
  70.6 0.0 all-to-all-done.1.recv_ref
  70.6 8.3 %second_halo.1 = bf16[12,512,128]{2,1,0:T(8,128)(2,1)} custom-call(s32[12,27]{1,0:T(8,128)} %src_ref.3, f32[6,512,256]{2,1,0:T(8,128)} %get-tuple-element.26.part_ref, bf16[12,512,128]{2,1,0:T(8,128)(2,1)} %get-tuple-element.19.mask_ref, bf16[27,128,128]{2,1,0:T(8,128)(2,1)} %w_ref.7, bf16[12,304,128]{2,1,0:T(8,128)(2,1)} %get-tuple-element.27.shells_ref, ...), custom_call_target="tpu_custom_call" | custom-call | flops 1811939328 | bytes 10485760 | tf_op jit(solution)/shard_map/second_halo/pallas_call | solution.py:543
Async XLA Ops:
  4.7 29.4 %all-to-all-start = ((bf16[16,304,128]{2,1,0:T(8,128)(2,1)}), bf16[16,304,128]{2,1,0:T(8,128)(2,1)}, u32[]{:S(2)}, u32[]{:S(2)}) async-start(bf16[16,304,128]{2,1,0:T(8,128)(2,1)} %get-tuple-element.23), calls=%async_computation | async-start | bytes 2490368 | tf_op jit(solution)/shard_map/all_to_all | solution.py:564
  11.5 21.5 %collective-permute-start = (bf16[2,304,128]{2,1,0:T(8,128)(2,1)}, bf16[2,304,128]{2,1,0:T(8,128)(2,1)}, u32[]{:S(2)}, u32[]{:S(2)}) collective-permute-start(bf16[2,304,128]{2,1,0:T(8,128)(2,1)} %get-tuple-element.21), channel_id=1, source_target_pairs={{0,1},{1,0},{2,3},{3,2},{4,5},{5,4},{6,7},{7,6},{8,9},{9,8},{10,11... | collective-permute-start | bytes 466952 | tf_op jit(solution)/shard_map/ppermute | solution.py:560
  12.8 21.3 %collective-permute-start.1 = (bf16[2,304,128]{2,1,0:T(8,128)(2,1)}, bf16[2,304,128]{2,1,0:T(8,128)(2,1)}, u32[]{:S(2)}, u32[]{:S(2)}) collective-permute-start(bf16[2,304,128]{2,1,0:T(8,128)(2,1)} %get-tuple-element.22), channel_id=1, source_target_pairs={{1,2},{2,1},{3,4},{4,3},{5,6},{6,5},{7,8},{8,7},{9,10},{10,9},{11,... | collective-permute-start | bytes 466952 | tf_op jit(solution)/shard_map/ppermute | solution.py:560
  43.5 27.1 %all-to-all-start.1 = ((bf16[16,304,128]{2,1,0:T(8,128)(2,1)}), bf16[16,304,128]{2,1,0:T(8,128)(2,1)}, u32[]{:S(2)}, u32[]{:S(2)}) async-start(bf16[16,304,128]{2,1,0:T(8,128)(2,1)} %get-tuple-element.30), calls=%async_computation.1 | async-start | bytes 2490368 | tf_op jit(solution)/shard_map/all_to_all | solution.py:564
  47.9 19.7 %collective-permute-start.2 = (bf16[2,304,128]{2,1,0:T(8,128)(2,1)}, bf16[2,304,128]{2,1,0:T(8,128)(2,1)}, u32[]{:S(2)}, u32[]{:S(2)}) collective-permute-start(bf16[2,304,128]{2,1,0:T(8,128)(2,1)} %get-tuple-element.28), channel_id=1, source_target_pairs={{0,1},{1,0},{2,3},{3,2},{4,5},{5,4},{6,7},{7,6},{8,9},{9,8},{10,11... | collective-permute-start | bytes 466952 | tf_op jit(solution)/shard_map/ppermute | solution.py:560
  49.1 21.5 %collective-permute-start.3 = (bf16[2,304,128]{2,1,0:T(8,128)(2,1)}, bf16[2,304,128]{2,1,0:T(8,128)(2,1)}, u32[]{:S(2)}, u32[]{:S(2)}) collective-permute-start(bf16[2,304,128]{2,1,0:T(8,128)(2,1)} %get-tuple-element.29), channel_id=1, source_target_pairs={{1,2},{2,1},{3,4},{4,3},{5,6},{6,5},{7,8},{8,7},{9,10},{10,9},{11,... | collective-permute-start | bytes 466952 | tf_op jit(solution)/shard_map/ppermute | solution.py:560

commit v3 on v2

--- a/solution.py
+++ b/solution.py
@@ -143,18 +143,10 @@
     return jnp.where(last, fill, pltpu.roll(value, 7, 0))
 
 
-def own_conv(plane, w_ref, part_ref, wide, block, base=None):
-    step = pl.program_id(0)
-
-    @pl.when(step == 0)
-    def _():
-        block[...] = jnp.zeros_like(block)
-        for tap in range(9):
-            toeplitz(wide.at[tap], (w_ref[tap], w_ref[9 + tap], w_ref[18 + tap]))
-
+def own_pair(pair, plane, part_ref, wide, block, base):
     first, last = edge_masks()
     for x in range(8):
-        planes = [plane(half, x) for half in range(2)]
+        planes = [plane(2 * pair + half, x) for half in range(2)]
         px = x + 1
         lanes = slice((px % 2) * 128, (px % 2) * 128 + 128)
         for y in range(8):
@@ -174,15 +166,28 @@
                 part = block[az, side : side + 4, ay : ay + 8].reshape(512, 256)
                 acc = acc + jnp.dot(part, wide[ay * 3 + az, side], preferred_element_type=jnp.float32)
     if base is None:
-        part_ref[0] = acc
+        part_ref[pair] = acc
         return
     for half in range(2):
         for x in range(8):
-            added = base(half, x)
+            added = base(2 * pair + half, x)
             lanes = slice((x % 2) * 128, (x % 2) * 128 + 128)
             for y in range(8):
                 row = (x // 2) * 128 + y * 16 + half * 8
-                part_ref[0, row : row + 8, lanes] = acc[row : row + 8, lanes] + added[y * 8 : y * 8 + 8]
+                part_ref[pair, row : row + 8, lanes] = acc[row : row + 8, lanes] + added[y * 8 : y * 8 + 8]
+
+
+def own_conv(plane, w_ref, part_ref, wide, block, base=None):
+    step = pl.program_id(0)
+
+    @pl.when(step == 0)
+    def _():
+        block[...] = jnp.zeros_like(block)
+        for tap in range(9):
+            toeplitz(wide.at[tap], (w_ref[tap], w_ref[9 + tap], w_ref[18 + tap]))
+
+    for pair in range(STEP // 2):
+        own_pair(pair, plane, part_ref, wide, block.at[pair], base)
 
 
 def first_own_kernel(feat_ref, occ_ref, w_ref, part_ref, x_ref, mask_ref, shell_ref, wide, block, cells, inner):
@@ -192,8 +197,8 @@
     diagonal = rows == cols
     ones = jnp.ones((128, 128), jnp.bfloat16)
     held = {}
-    for half in range(2):
-        occupied = occ_ref[pl.ds(step * 2 + half, 1), :].astype(jnp.float32)
+    for half in range(STEP):
+        occupied = occ_ref[pl.ds(step * STEP + half, 1), :].astype(jnp.float32)
         for chunk in range(4):
             at = slice(chunk * 128, chunk * 128 + 128)
             scale = jnp.where(diagonal, jnp.broadcast_to(occupied[:, at], (128, 128)), 0.0).astype(jnp.bfloat16)
@@ -211,7 +216,7 @@
 
 def second_own_kernel(hidden_ref, x_ref, w_ref, part_ref, shell_ref, wide, block, cells, inner):
     plane = lambda ref: lambda half, x: ref[half, x * 64 : x * 64 + 64, :].astype(jnp.float32)
-    for half in range(2):
+    for half in range(STEP):
         planes = [plane(hidden_ref)(half, x) for x in range(8)]
         store_shell(shell_ref.at[half], planes)
         store_inner(shell_ref.at[half], planes, cells.at[half], inner.at[half])
@@ -274,13 +279,15 @@
                 put(pair, x + 1, [z_plane(here[half], x) for half in range(2)])
 
 
-def halo_weights(w_ref, along):
-    for face in range(2):
-        end = 2 * face
-        for shift in range(3):
-            toeplitz(along.at[face, shift], [w_ref[end * 9 + tap * 3 + shift] for tap in range(3)])
-            toeplitz(along.at[2 + face, shift], [w_ref[tap * 9 + end * 3 + shift] for tap in range(3)])
-            toeplitz(along.at[4 + face, shift], [w_ref[tap * 9 + shift * 3 + end] for tap in range(3)])
+def face_weights(face, w, along):
+    end = 2 * (face % 2)
+    for shift in range(3):
+        taps = (
+            [end * 9 + tap * 3 + shift for tap in range(3)],
+            [tap * 9 + end * 3 + shift for tap in range(3)],
+            [tap * 9 + shift * 3 + end for tap in range(3)],
+        )[face // 2]
+        toeplitz(along.at[face, shift], [w[tap] for tap in taps])
 
 
 def sum_face(face, halo, along, sums):
@@ -301,18 +308,19 @@
             halo[face, shift, 0, :, 0:128] = jnp.zeros((8 * BR, 128), jnp.bfloat16)
             halo[face, shift, 4, :, 128:256] = jnp.zeros((8 * BR, 128), jnp.bfloat16)
     near, far = BR + EDGE * (1 - odd), BR + EDGE * odd
-    loads[0].wait()
-    halo_weights(landed[0], along)
-    for load, start, field in zip(loads[1:], (0, near, far, BR + 2 * EDGE), landed[1:]):
+    for load, start, field in zip(loads[:4], (0, near, far, BR + 2 * EDGE), landed[:4]):
         load.wait()
-        if field is landed[-1]:
+        if field is landed[3]:
             start_streams(streams, stream_sems)
         fill_pool(pool, start, field)
 
     build_face(0, src_ref, pool, halo)
+    loads[4].wait()
+    face_weights(0, landed[4], along)
     for face in range(6):
         if face < 5:
             build_face(face + 1, src_ref, pool, halo)
+            face_weights(face + 1, landed[4], along)
         sum_face(face, halo, along, sums)
 
 
@@ -351,11 +359,11 @@
     src_ref, send_ref, pick_ref, part_ref, mask_ref, w_ref, shells_ref, near_in_ref, far_in_ref, recv_ref,
     hidden_ref, out_ref, near_ref, far_ref,
     pool, halo, along, sums, w, shells, near, far, recv, part, mask, done, sems, stream_sems, done_sems,
-    own, out_sems,
+    own, out_sems, cells, inner,
 ):
     streams = ((part_ref, part, 1), (mask_ref, mask, 2))
-    sources = (w_ref, shells_ref, near_in_ref, far_in_ref, recv_ref)
-    landed = (w, shells, near, far, recv)
+    sources = (shells_ref, near_in_ref, far_in_ref, recv_ref, w_ref)
+    landed = (shells, near, far, recv, w)
     halo_part(parity(), src_ref, sources, landed, sems, streams, stream_sems, pool, halo, along, sums)
 
     def store(pair):
@@ -374,15 +382,11 @@
                 done[brick, rows, :] = value.astype(jnp.bfloat16)
                 planes.append(value)
             store_shell(own.at[brick], planes)
+            store_inner(own.at[brick], planes, cells.at[half], inner.at[half])
         store(pair).start()
         return carry
 
     lax.fori_loop(0, BR // 2, pair_body, 0)
-    for brick in range(0, BR, 2):
-        both = jnp.concatenate([done[brick], done[brick + 1]], axis=1)
-        inner = jnp.dot(pick_ref[...], both, preferred_element_type=jnp.float32).astype(jnp.bfloat16)
-        own[brick, FACE_LO:SHELL, :] = inner[:, :128]
-        own[brick + 1, FACE_LO:SHELL, :] = inner[:, 128:]
     copies = hand_out(send_ref, parity(), own, out_ref, near_ref, far_ref, out_sems)
     wait_all([store(pair) for pair in range(BR // 2)])
     wait_all(copies)
@@ -394,8 +398,8 @@
     pool, halo, along, sums, w, shells, near, far, recv, part, mask, done, sems, stream_sems, done_sems,
 ):
     streams = ((part_ref, part, 1), (mask_ref, mask, 2))
-    sources = (w_ref, shells_ref, near_in_ref, far_in_ref, recv_ref)
-    landed = (w, shells, near, far, recv)
+    sources = (shells_ref, near_in_ref, far_in_ref, recv_ref, w_ref)
+    landed = (shells, near, far, recv, w)
     halo_part(parity(), src_ref, sources, landed, sems, streams, stream_sems, pool, halo, along, sums)
 
     def store(pair):
@@ -420,21 +424,22 @@
 WHOLE = functools.partial(pl.BlockSpec, memory_space=pltpu.VMEM)
 SCALARS = functools.partial(pl.BlockSpec, memory_space=pltpu.SMEM)
 ANYWHERE = functools.partial(pl.BlockSpec, memory_space=pl.ANY)
-GRID = (BR // 2,)
+STEP = 4
+GRID = (BR // STEP,)
 FIELD = jax.ShapeDtypeStruct((BR, 512, 128), jnp.bfloat16)
 PARTIAL = jax.ShapeDtypeStruct((BR // 2, 512, 256), jnp.float32)
 
 
 def pair_spec():
-    return pl.BlockSpec((2, 512, 128), lambda i: (i, 0, 0))
+    return pl.BlockSpec((STEP, 512, 128), lambda i: (i, 0, 0))
 
 
 def part_spec():
-    return pl.BlockSpec((1, 512, 256), lambda i: (i, 0, 0))
+    return pl.BlockSpec((STEP // 2, 512, 256), lambda i: (i, 0, 0))
 
 
 def shell_pair_spec():
-    return pl.BlockSpec((2, SHELL, 128), lambda i: (i, 0, 0))
+    return pl.BlockSpec((STEP, SHELL, 128), lambda i: (i, 0, 0))
 
 
 def shells_of(*counts):
@@ -448,9 +453,9 @@
 def own_scratch():
     return [
         pltpu.VMEM((9, 2, 256, 256), jnp.bfloat16),
-        pltpu.VMEM((3, 5, 10, 16, 256), jnp.bfloat16),
-        pltpu.VMEM((2, 512, 128), jnp.float32),
-        pltpu.VMEM((2, SHELL - FACE_LO, 128), jnp.float32),
+        pltpu.VMEM((STEP // 2, 3, 5, 10, 16, 256), jnp.bfloat16),
+        pltpu.VMEM((STEP, 512, 128), jnp.float32),
+        pltpu.VMEM((STEP, SHELL - FACE_LO, 128), jnp.float32),
     ]
 
 
@@ -532,7 +537,7 @@
         in_specs=[SCALARS(), SCALARS(), WHOLE()] + [ANYWHERE()] * 7,
         out_specs=[ANYWHERE()] * 4,
         out_shape=[FIELD] + shells_of(SLOTS, EDGE, EDGE),
-        scratch_shapes=halo_scratch() + own_shells_scratch(),
+        scratch_shapes=halo_scratch() + own_shells_scratch() + own_scratch()[2:],
         compiler_params=params(),
         cost_estimate=HALO_COST,
         name="first_halo",

time: 79.6 us -> 77.6 us (0.975)
  Pallas kernels: 46.9 us -> 44 us
  waiting for transfers between devices: 4.05 us -> 4.92 us
    pallas_call x1, Pallas kernels: 8.27 us -> 7.07 us  [second_halo(): pl.pallas_call(second_halo_kernel, in_specs=[SCALARS()] + [ANYWHERE()] *...]
    ppermute x4, waiting for transfers between devices: 4.04 us -> 4.92 us  [swapped(): return lax.ppermute(value, axes, routes)]
    pallas_call x1, Pallas kernels: 9.42 us -> 8.62 us  [first_halo(): pl.pallas_call(first_halo_kernel, in_specs=[SCALARS(), SCALARS(), WHOLE()...]
where the time goes in v3:
time: 77.6 us; the launch traced here: 77.1 us
  Pallas kernels  44 us (57%)
  starting transfers between devices  28 us (36%)
  waiting for transfers between devices  4.92 us (6%)
    ppermute x4, starting transfers between devices, swapped(): return lax.ppermute(value, axes, routes)  16.8 us
    pallas_call x1, Pallas kernels, first_own(): pl.pallas_call(first_own_kernel, grid=GRID, in_specs=[pair_spec(), WHOLE(...  12.3 us
    pallas_call x1, Pallas kernels, second_own(): pl.pallas_call(second_own_kernel, grid=GRID, in_specs=[pair_spec(), pair_...  11.3 us
    all_to_all x2, starting transfers between devices, exchange(): lax.all_to_all(outgoing, 'dev', split_axis=0, concat_axis=0, tiled=True)  11.2 us
    pallas_call x1, Pallas kernels, first_halo(): pl.pallas_call(first_halo_kernel, in_specs=[SCALARS(), SCALARS(), WHOLE()...  8.62 us
    pallas_call x1, Pallas kernels, second_halo(): pl.pallas_call(second_halo_kernel, in_specs=[SCALARS()] + [ANYWHERE()] *...  7.07 us
    ppermute x4, waiting for transfers between devices, swapped(): return lax.ppermute(value, axes, routes)  4.92 us
    pallas_call x1, Pallas kernels, pack(): pl.pallas_call(pack_kernel, in_specs=[SCALARS(), ANYWHERE(), WHOLE(), ANY...  4.69 us
  transfers between devices with their start and end apart: 6, of which 2 were waited for; matrix products, arithmetic and copies ran while one was open for 0% of the time, Pallas kernels for 31%

profile of v3, /device:TPU:65, one launch (start us, length us, event | category | flops | bytes accessed | tf_op | source)
XLA Modules:
  0.0 77.1 jit_solution(13144941897017357816)
XLA Ops:
  0.0 4.7 %pack_shells.1 = (bf16[16,304,128]{2,1,0:T(8,128)(2,1)}, bf16[2,304,128]{2,1,0:T(8,128)(2,1)}, bf16[2,304,128]{2,1,0:T(8,128)(2,1)}) custom-call(s32[16]{0:T(128)} %bitcast.1, bf16[12,512,128]{2,1,0:T(8,128)(2,1)} %feat_ref.3, s32[12,512]{1,0:T(8,128)} %occ_ref.3, bf16[304,512]{1,0:T(8,128)(2,1)} %constant.2.clone.pick_ref), custom_call_target="tpu_custom_call" | custom-call | tf_op jit(solution)/shard_map/pack_shells/pallas_call | solution.py:489
  4.7 6.8 %all-to-all-start = ((bf16[16,304,128]{2,1,0:T(8,128)(2,1)}), bf16[16,304,128]{2,1,0:T(8,128)(2,1)}, u32[]{:S(2)}, u32[]{:S(2)}) async-start(bf16[16,304,128]{2,1,0:T(8,128)(2,1)} %get-tuple-element.23), calls=%async_computation | async-start | bytes 2490368 | tf_op jit(solution)/shard_map/all_to_all | solution.py:569
  11.5 1.3 %collective-permute-start = (bf16[2,304,128]{2,1,0:T(8,128)(2,1)}, bf16[2,304,128]{2,1,0:T(8,128)(2,1)}, u32[]{:S(2)}, u32[]{:S(2)}) collective-permute-start(bf16[2,304,128]{2,1,0:T(8,128)(2,1)} %get-tuple-element.21), channel_id=1, source_target_pairs={{0,1},{1,0},{2,3},{3,2},{4,5},{5,4},{6,7},{7,6},{8,9},{9,8},{10,11... | collective-permute-start | bytes 466952 | tf_op jit(solution)/shard_map/ppermute | solution.py:565
  12.8 7.2 %collective-permute-start.1 = (bf16[2,304,128]{2,1,0:T(8,128)(2,1)}, bf16[2,304,128]{2,1,0:T(8,128)(2,1)}, u32[]{:S(2)}, u32[]{:S(2)}) collective-permute-start(bf16[2,304,128]{2,1,0:T(8,128)(2,1)} %get-tuple-element.22), channel_id=1, source_target_pairs={{1,2},{2,1},{3,4},{4,3},{5,6},{6,5},{7,8},{8,7},{9,10},{10,9},{11,... | collective-permute-start | bytes 466952 | tf_op jit(solution)/shard_map/ppermute | solution.py:565
  20.0 12.3 %first_own.1 = (f32[6,512,256]{2,1,0:T(8,128)}, bf16[12,512,128]{2,1,0:T(8,128)(2,1)}, bf16[12,512,128]{2,1,0:T(8,128)(2,1)}, bf16[12,304,128]{2,1,0:T(8,128)(2,1)}) custom-call(bf16[12,512,128]{2,1,0:T(8,128)(2,1)} %feat_ref.3, s32[12,512]{1,0:T(8,128)} %occ_ref.3, bf16[27,128,128]{2,1,0:T(8,128)(2,1)} %w_ref.5), custom_call_target="tpu_custom_call" | custom-call | flops 7247757312 | bytes 8388608 | tf_op jit(solution)/shard_map/first_own/pallas_call | solution.py:507
  32.3 0.0 collective-permute-done.near_in_ref
  32.3 1.8 %collective-permute-done.1.far_in_ref = bf16[2,304,128]{2,1,0:T(8,128)(2,1)} collective-permute-done((bf16[2,304,128]{2,1,0:T(8,128)(2,1)}, bf16[2,304,128]{2,1,0:T(8,128)(2,1)}, u32[]{:S(2)}, u32[]{:S(2)}) %collective-permute-start.1) | collective-permute-done | bytes 155680 | tf_op jit(solution)/shard_map/ppermute | solution.py:565
  34.1 0.0 all-to-all-done.recv_ref
  34.1 8.6 %first_halo.1 = (bf16[12,512,128]{2,1,0:T(8,128)(2,1)}, bf16[16,304,128]{2,1,0:T(8,128)(2,1)}, bf16[2,304,128]{2,1,0:T(8,128)(2,1)}, bf16[2,304,128]{2,1,0:T(8,128)(2,1)}) custom-call(s32[12,27]{1,0:T(8,128)} %src_ref.3, s32[16]{0:T(128)} %bitcast.2, bf16[80,512]{1,0:T(8,128)(2,1)} %constant.7.pick_ref, f32[6,512,256]{2,1,0:T(8,128)} %get-tuple-element.18.part_ref, ...), custom_call_target="tpu_custom_call" | custom-call | flops 1811939328 | bytes 10485760 | tf_op jit(solution)/shard_map/first_halo/pallas_call | solution.py:535
  42.7 4.4 %all-to-all-start.1 = ((bf16[16,304,128]{2,1,0:T(8,128)(2,1)}), bf16[16,304,128]{2,1,0:T(8,128)(2,1)}, u32[]{:S(2)}, u32[]{:S(2)}) async-start(bf16[16,304,128]{2,1,0:T(8,128)(2,1)} %get-tuple-element.30), calls=%async_computation.1 | async-start | bytes 2490368 | tf_op jit(solution)/shard_map/all_to_all | solution.py:569
  47.1 1.2 %collective-permute-start.2 = (bf16[2,304,128]{2,1,0:T(8,128)(2,1)}, bf16[2,304,128]{2,1,0:T(8,128)(2,1)}, u32[]{:S(2)}, u32[]{:S(2)}) collective-permute-start(bf16[2,304,128]{2,1,0:T(8,128)(2,1)} %get-tuple-element.28), channel_id=1, source_target_pairs={{0,1},{1,0},{2,3},{3,2},{4,5},{5,4},{6,7},{7,6},{8,9},{9,8},{10,11... | collective-permute-start | bytes 466952 | tf_op jit(solution)/shard_map/ppermute | solution.py:565
  48.3 7.0 %collective-permute-start.3 = (bf16[2,304,128]{2,1,0:T(8,128)(2,1)}, bf16[2,304,128]{2,1,0:T(8,128)(2,1)}, u32[]{:S(2)}, u32[]{:S(2)}) collective-permute-start(bf16[2,304,128]{2,1,0:T(8,128)(2,1)} %get-tuple-element.29), channel_id=1, source_target_pairs={{1,2},{2,1},{3,4},{4,3},{5,6},{6,5},{7,8},{8,7},{9,10},{10,9},{11,... | collective-permute-start | bytes 466952 | tf_op jit(solution)/shard_map/ppermute | solution.py:565
  55.4 11.3 %second_own.1 = (f32[6,512,256]{2,1,0:T(8,128)}, bf16[12,304,128]{2,1,0:T(8,128)(2,1)}) custom-call(bf16[12,512,128]{2,1,0:T(8,128)(2,1)} %get-tuple-element.24.hidden_ref, bf16[12,512,128]{2,1,0:T(8,128)(2,1)} %get-tuple-element.25.x_ref, bf16[27,128,128]{2,1,0:T(8,128)(2,1)} %w_ref.7), custom_call_target="tpu_custom_call" | custom-call | flops 7247757312 | bytes 8388608 | tf_op jit(solution)/shard_map/second_own/pallas_call | solution.py:521
  66.7 0.0 collective-permute-done.2.near_in_ref
  66.7 3.1 %collective-permute-done.3.far_in_ref = bf16[2,304,128]{2,1,0:T(8,128)(2,1)} collective-permute-done((bf16[2,304,128]{2,1,0:T(8,128)(2,1)}, bf16[2,304,128]{2,1,0:T(8,128)(2,1)}, u32[]{:S(2)}, u32[]{:S(2)}) %collective-permute-start.3) | collective-permute-done | bytes 155680 | tf_op jit(solution)/shard_map/ppermute | solution.py:565
  69.8 0.0 all-to-all-done.1.recv_ref
  69.8 7.1 %second_halo.1 = bf16[12,512,128]{2,1,0:T(8,128)(2,1)} custom-call(s32[12,27]{1,0:T(8,128)} %src_ref.3, f32[6,512,256]{2,1,0:T(8,128)} %get-tuple-element.26.part_ref, bf16[12,512,128]{2,1,0:T(8,128)(2,1)} %get-tuple-element.19.mask_ref, bf16[27,128,128]{2,1,0:T(8,128)(2,1)} %w_ref.7, bf16[12,304,128]{2,1,0:T(8,128)(2,1)} %get-tuple-element.27.shells_ref, ...), custom_call_target="tpu_custom_call" | custom-call | flops 1811939328 | bytes 10485760 | tf_op jit(solution)/shard_map/second_halo/pallas_call | solution.py:548
Async XLA Ops:
  4.7 29.4 %all-to-all-start = ((bf16[16,304,128]{2,1,0:T(8,128)(2,1)}), bf16[16,304,128]{2,1,0:T(8,128)(2,1)}, u32[]{:S(2)}, u32[]{:S(2)}) async-start(bf16[16,304,128]{2,1,0:T(8,128)(2,1)} %get-tuple-element.23), calls=%async_computation | async-start | bytes 2490368 | tf_op jit(solution)/shard_map/all_to_all | solution.py:569
  11.5 20.8 %collective-permute-start = (bf16[2,304,128]{2,1,0:T(8,128)(2,1)}, bf16[2,304,128]{2,1,0:T(8,128)(2,1)}, u32[]{:S(2)}, u32[]{:S(2)}) collective-permute-start(bf16[2,304,128]{2,1,0:T(8,128)(2,1)} %get-tuple-element.21), channel_id=1, source_target_pairs={{0,1},{1,0},{2,3},{3,2},{4,5},{5,4},{6,7},{7,6},{8,9},{9,8},{10,11... | collective-permute-start | bytes 466952 | tf_op jit(solution)/shard_map/ppermute | solution.py:565
  12.8 21.3 %collective-permute-start.1 = (bf16[2,304,128]{2,1,0:T(8,128)(2,1)}, bf16[2,304,128]{2,1,0:T(8,128)(2,1)}, u32[]{:S(2)}, u32[]{:S(2)}) collective-permute-start(bf16[2,304,128]{2,1,0:T(8,128)(2,1)} %get-tuple-element.22), channel_id=1, source_target_pairs={{1,2},{2,1},{3,4},{4,3},{5,6},{6,5},{7,8},{8,7},{9,10},{10,9},{11,... | collective-permute-start | bytes 466952 | tf_op jit(solution)/shard_map/ppermute | solution.py:565
  42.7 27.1 %all-to-all-start.1 = ((bf16[16,304,128]{2,1,0:T(8,128)(2,1)}), bf16[16,304,128]{2,1,0:T(8,128)(2,1)}, u32[]{:S(2)}, u32[]{:S(2)}) async-start(bf16[16,304,128]{2,1,0:T(8,128)(2,1)} %get-tuple-element.30), calls=%async_computation.1 | async-start | bytes 2490368 | tf_op jit(solution)/shard_map/all_to_all | solution.py:569
  47.1 19.5 %collective-permute-start.2 = (bf16[2,304,128]{2,1,0:T(8,128)(2,1)}, bf16[2,304,128]{2,1,0:T(8,128)(2,1)}, u32[]{:S(2)}, u32[]{:S(2)}) collective-permute-start(bf16[2,304,128]{2,1,0:T(8,128)(2,1)} %get-tuple-element.28), channel_id=1, source_target_pairs={{0,1},{1,0},{2,3},{3,2},{4,5},{5,4},{6,7},{7,6},{8,9},{9,8},{10,11... | collective-permute-start | bytes 466952 | tf_op jit(solution)/shard_map/ppermute | solution.py:565
  48.3 21.5 %collective-permute-start.3 = (bf16[2,304,128]{2,1,0:T(8,128)(2,1)}, bf16[2,304,128]{2,1,0:T(8,128)(2,1)}, u32[]{:S(2)}, u32[]{:S(2)}) collective-permute-start(bf16[2,304,128]{2,1,0:T(8,128)(2,1)} %get-tuple-element.29), channel_id=1, source_target_pairs={{1,2},{2,1},{3,4},{4,3},{5,6},{6,5},{7,8},{8,7},{9,10},{10,9},{11,... | collective-permute-start | bytes 466952 | tf_op jit(solution)/shard_map/ppermute | solution.py:565

commit v4 on v3

--- a/solution.py
+++ b/solution.py
@@ -87,14 +87,26 @@
         copy.wait()
 
 
-def hand_out(send_ref, odd, own, out_ref, near_ref, far_ref, sems):
+def send_below(send_ref, own, out_ref, sems, begin, end):
+    for slot in range(SLOTS):
+        brick = jnp.maximum(send_ref[slot], 0)
+
+        @pl.when((brick >= begin) & (brick < end))
+        def _():
+            pltpu.make_async_copy(own.at[brick], out_ref.at[slot], sems.at[slot]).start()
+
+
+def hand_out(send_ref, odd, own, out_ref, near_ref, far_ref, sems, slots_too=True):
     first, second = jnp.where(odd == 0, BR - EDGE, 0), jnp.where(odd == 0, 0, BR - EDGE)
     copies = [pltpu.make_async_copy(own.at[pl.ds(first, EDGE)], near_ref, sems.at[SLOTS])]
     copies.append(pltpu.make_async_copy(own.at[pl.ds(second, EDGE)], far_ref, sems.at[SLOTS + 1]))
+    start_all(copies)
     for slot in range(SLOTS):
         brick = jnp.maximum(send_ref[slot], 0)
         copies.append(pltpu.make_async_copy(own.at[brick], out_ref.at[slot], sems.at[slot]))
-    return start_all(copies)
+        if slots_too:
+            copies[-1].start()
+    return copies
 
 
 def pack_kernel(
@@ -114,7 +126,8 @@
             chooser = pick[...] * jnp.broadcast_to(held, (SHELL, 512))
             shell = jnp.dot(chooser, feats[brick], preferred_element_type=jnp.float32)
             own[brick] = shell.astype(jnp.bfloat16)
-    wait_all(hand_out(send_ref, parity(), own, out_ref, near_ref, far_ref, out_sems))
+        send_below(send_ref, own, out_ref, out_sems, 2 * part, 2 * part + 6)
+    wait_all(hand_out(send_ref, parity(), own, out_ref, near_ref, far_ref, out_sems, False))
 
 
 def toeplitz(target, taps):
@@ -386,8 +399,11 @@
         store(pair).start()
         return carry
 
-    lax.fori_loop(0, BR // 2, pair_body, 0)
-    copies = hand_out(send_ref, parity(), own, out_ref, near_ref, far_ref, out_sems)
+    lax.fori_loop(0, BR // 4, pair_body, 0)
+    send_below(send_ref, own, out_ref, out_sems, 0, BR // 2)
+    lax.fori_loop(BR // 4, BR // 2, pair_body, 0)
+    send_below(send_ref, own, out_ref, out_sems, BR // 2, BR)
+    copies = hand_out(send_ref, parity(), own, out_ref, near_ref, far_ref, out_sems, False)
     wait_all([store(pair) for pair in range(BR // 2)])
     wait_all(copies)
 

time: 77.6 us -> 77.2 us (level)
  no operation moved by 1% of the time
where the time goes in v4:
time: 77.2 us; the launch traced here: 76.6 us
  Pallas kernels  43.5 us (56%)
  starting transfers between devices  28 us (36%)
  waiting for transfers between devices  4.96 us (6%)
    ppermute x4, starting transfers between devices, swapped(): return lax.ppermute(value, axes, routes)  16.7 us
    pallas_call x1, Pallas kernels, first_own(): pl.pallas_call(first_own_kernel, grid=GRID, in_specs=[pair_spec(), WHOLE(...  12.3 us
    pallas_call x1, Pallas kernels, second_own(): pl.pallas_call(second_own_kernel, grid=GRID, in_specs=[pair_spec(), pair_...  11.3 us
    all_to_all x2, starting transfers between devices, exchange(): lax.all_to_all(outgoing, 'dev', split_axis=0, concat_axis=0, tiled=True)  11.3 us
    pallas_call x1, Pallas kernels, first_halo(): pl.pallas_call(first_halo_kernel, in_specs=[SCALARS(), SCALARS(), WHOLE()...  8.41 us
    pallas_call x1, Pallas kernels, second_halo(): pl.pallas_call(second_halo_kernel, in_specs=[SCALARS()] + [ANYWHERE()] *...  7.05 us
    ppermute x4, waiting for transfers between devices, swapped(): return lax.ppermute(value, axes, routes)  4.95 us
    pallas_call x1, Pallas kernels, pack(): pl.pallas_call(pack_kernel, in_specs=[SCALARS(), ANYWHERE(), WHOLE(), ANY...  4.42 us
  transfers between devices with their start and end apart: 6, of which 2 were waited for; matrix products, arithmetic and copies ran while one was open for 0% of the time, Pallas kernels for 31%

profile of v4, /device:TPU:65, one launch (start us, length us, event | category | flops | bytes accessed | tf_op | source)
XLA Modules:
  0.0 76.6 jit_solution(15314135237212581621)
XLA Ops:
  0.0 4.4 %pack_shells.1 = (bf16[16,304,128]{2,1,0:T(8,128)(2,1)}, bf16[2,304,128]{2,1,0:T(8,128)(2,1)}, bf16[2,304,128]{2,1,0:T(8,128)(2,1)}) custom-call(s32[16]{0:T(128)} %bitcast.1, bf16[12,512,128]{2,1,0:T(8,128)(2,1)} %feat_ref.3, s32[12,512]{1,0:T(8,128)} %occ_ref.3, bf16[304,512]{1,0:T(8,128)(2,1)} %constant.2.clone.pick_ref), custom_call_target="tpu_custom_call" | custom-call | tf_op jit(solution)/shard_map/pack_shells/pallas_call | solution.py:505
  4.4 6.9 %all-to-all-start = ((bf16[16,304,128]{2,1,0:T(8,128)(2,1)}), bf16[16,304,128]{2,1,0:T(8,128)(2,1)}, u32[]{:S(2)}, u32[]{:S(2)}) async-start(bf16[16,304,128]{2,1,0:T(8,128)(2,1)} %get-tuple-element.23), calls=%async_computation | async-start | bytes 2490368 | tf_op jit(solution)/shard_map/all_to_all | solution.py:585
  11.3 1.3 %collective-permute-start = (bf16[2,304,128]{2,1,0:T(8,128)(2,1)}, bf16[2,304,128]{2,1,0:T(8,128)(2,1)}, u32[]{:S(2)}, u32[]{:S(2)}) collective-permute-start(bf16[2,304,128]{2,1,0:T(8,128)(2,1)} %get-tuple-element.21), channel_id=1, source_target_pairs={{0,1},{1,0},{2,3},{3,2},{4,5},{5,4},{6,7},{7,6},{8,9},{9,8},{10,11... | collective-permute-start | bytes 466952 | tf_op jit(solution)/shard_map/ppermute | solution.py:581
  12.6 7.2 %collective-permute-start.1 = (bf16[2,304,128]{2,1,0:T(8,128)(2,1)}, bf16[2,304,128]{2,1,0:T(8,128)(2,1)}, u32[]{:S(2)}, u32[]{:S(2)}) collective-permute-start(bf16[2,304,128]{2,1,0:T(8,128)(2,1)} %get-tuple-element.22), channel_id=1, source_target_pairs={{1,2},{2,1},{3,4},{4,3},{5,6},{6,5},{7,8},{8,7},{9,10},{10,9},{11,... | collective-permute-start | bytes 466952 | tf_op jit(solution)/shard_map/ppermute | solution.py:581
  19.8 12.3 %first_own.1 = (f32[6,512,256]{2,1,0:T(8,128)}, bf16[12,512,128]{2,1,0:T(8,128)(2,1)}, bf16[12,512,128]{2,1,0:T(8,128)(2,1)}, bf16[12,304,128]{2,1,0:T(8,128)(2,1)}) custom-call(bf16[12,512,128]{2,1,0:T(8,128)(2,1)} %feat_ref.3, s32[12,512]{1,0:T(8,128)} %occ_ref.3, bf16[27,128,128]{2,1,0:T(8,128)(2,1)} %w_ref.5), custom_call_target="tpu_custom_call" | custom-call | flops 7247757312 | bytes 8388608 | tf_op jit(solution)/shard_map/first_own/pallas_call | solution.py:523
  32.1 0.0 collective-permute-done.near_in_ref
  32.1 1.8 %collective-permute-done.1.far_in_ref = bf16[2,304,128]{2,1,0:T(8,128)(2,1)} collective-permute-done((bf16[2,304,128]{2,1,0:T(8,128)(2,1)}, bf16[2,304,128]{2,1,0:T(8,128)(2,1)}, u32[]{:S(2)}, u32[]{:S(2)}) %collective-permute-start.1) | collective-permute-done | bytes 155680 | tf_op jit(solution)/shard_map/ppermute | solution.py:581
  33.9 0.0 all-to-all-done.recv_ref
  33.9 8.4 %first_halo.1 = (bf16[12,512,128]{2,1,0:T(8,128)(2,1)}, bf16[16,304,128]{2,1,0:T(8,128)(2,1)}, bf16[2,304,128]{2,1,0:T(8,128)(2,1)}, bf16[2,304,128]{2,1,0:T(8,128)(2,1)}) custom-call(s32[12,27]{1,0:T(8,128)} %src_ref.3, s32[16]{0:T(128)} %bitcast.2, bf16[80,512]{1,0:T(8,128)(2,1)} %constant.7.pick_ref, f32[6,512,256]{2,1,0:T(8,128)} %get-tuple-element.18.part_ref, ...), custom_call_target="tpu_custom_call" | custom-call | flops 1811939328 | bytes 10485760 | tf_op jit(solution)/shard_map/first_halo/pallas_call | solution.py:551
  42.3 4.4 %all-to-all-start.1 = ((bf16[16,304,128]{2,1,0:T(8,128)(2,1)}), bf16[16,304,128]{2,1,0:T(8,128)(2,1)}, u32[]{:S(2)}, u32[]{:S(2)}) async-start(bf16[16,304,128]{2,1,0:T(8,128)(2,1)} %get-tuple-element.30), calls=%async_computation.1 | async-start | bytes 2490368 | tf_op jit(solution)/shard_map/all_to_all | solution.py:585
  46.7 1.2 %collective-permute-start.2 = (bf16[2,304,128]{2,1,0:T(8,128)(2,1)}, bf16[2,304,128]{2,1,0:T(8,128)(2,1)}, u32[]{:S(2)}, u32[]{:S(2)}) collective-permute-start(bf16[2,304,128]{2,1,0:T(8,128)(2,1)} %get-tuple-element.28), channel_id=1, source_target_pairs={{0,1},{1,0},{2,3},{3,2},{4,5},{5,4},{6,7},{7,6},{8,9},{9,8},{10,11... | collective-permute-start | bytes 466952 | tf_op jit(solution)/shard_map/ppermute | solution.py:581
  47.9 7.0 %collective-permute-start.3 = (bf16[2,304,128]{2,1,0:T(8,128)(2,1)}, bf16[2,304,128]{2,1,0:T(8,128)(2,1)}, u32[]{:S(2)}, u32[]{:S(2)}) collective-permute-start(bf16[2,304,128]{2,1,0:T(8,128)(2,1)} %get-tuple-element.29), channel_id=1, source_target_pairs={{1,2},{2,1},{3,4},{4,3},{5,6},{6,5},{7,8},{8,7},{9,10},{10,9},{11,... | collective-permute-start | bytes 466952 | tf_op jit(solution)/shard_map/ppermute | solution.py:581
  55.0 11.3 %second_own.1 = (f32[6,512,256]{2,1,0:T(8,128)}, bf16[12,304,128]{2,1,0:T(8,128)(2,1)}) custom-call(bf16[12,512,128]{2,1,0:T(8,128)(2,1)} %get-tuple-element.24.hidden_ref, bf16[12,512,128]{2,1,0:T(8,128)(2,1)} %get-tuple-element.25.x_ref, bf16[27,128,128]{2,1,0:T(8,128)(2,1)} %w_ref.7), custom_call_target="tpu_custom_call" | custom-call | flops 7247757312 | bytes 8388608 | tf_op jit(solution)/shard_map/second_own/pallas_call | solution.py:537
  66.3 0.0 collective-permute-done.2.near_in_ref
  66.3 3.2 %collective-permute-done.3.far_in_ref = bf16[2,304,128]{2,1,0:T(8,128)(2,1)} collective-permute-done((bf16[2,304,128]{2,1,0:T(8,128)(2,1)}, bf16[2,304,128]{2,1,0:T(8,128)(2,1)}, u32[]{:S(2)}, u32[]{:S(2)}) %collective-permute-start.3) | collective-permute-done | bytes 155680 | tf_op jit(solution)/shard_map/ppermute | solution.py:581
  69.4 0.0 all-to-all-done.1.recv_ref
  69.4 7.0 %second_halo.1 = bf16[12,512,128]{2,1,0:T(8,128)(2,1)} custom-call(s32[12,27]{1,0:T(8,128)} %src_ref.3, f32[6,512,256]{2,1,0:T(8,128)} %get-tuple-element.26.part_ref, bf16[12,512,128]{2,1,0:T(8,128)(2,1)} %get-tuple-element.19.mask_ref, bf16[27,128,128]{2,1,0:T(8,128)(2,1)} %w_ref.7, bf16[12,304,128]{2,1,0:T(8,128)(2,1)} %get-tuple-element.27.shells_ref, ...), custom_call_target="tpu_custom_call" | custom-call | flops 1811939328 | bytes 10485760 | tf_op jit(solution)/shard_map/second_halo/pallas_call | solution.py:564
Async XLA Ops:
  4.4 29.5 %all-to-all-start = ((bf16[16,304,128]{2,1,0:T(8,128)(2,1)}), bf16[16,304,128]{2,1,0:T(8,128)(2,1)}, u32[]{:S(2)}, u32[]{:S(2)}) async-start(bf16[16,304,128]{2,1,0:T(8,128)(2,1)} %get-tuple-element.23), calls=%async_computation | async-start | bytes 2490368 | tf_op jit(solution)/shard_map/all_to_all | solution.py:585
  11.3 20.8 %collective-permute-start = (bf16[2,304,128]{2,1,0:T(8,128)(2,1)}, bf16[2,304,128]{2,1,0:T(8,128)(2,1)}, u32[]{:S(2)}, u32[]{:S(2)}) collective-permute-start(bf16[2,304,128]{2,1,0:T(8,128)(2,1)} %get-tuple-element.21), channel_id=1, source_target_pairs={{0,1},{1,0},{2,3},{3,2},{4,5},{5,4},{6,7},{7,6},{8,9},{9,8},{10,11... | collective-permute-start | bytes 466952 | tf_op jit(solution)/shard_map/ppermute | solution.py:581
  12.6 21.3 %collective-permute-start.1 = (bf16[2,304,128]{2,1,0:T(8,128)(2,1)}, bf16[2,304,128]{2,1,0:T(8,128)(2,1)}, u32[]{:S(2)}, u32[]{:S(2)}) collective-permute-start(bf16[2,304,128]{2,1,0:T(8,128)(2,1)} %get-tuple-element.22), channel_id=1, source_target_pairs={{1,2},{2,1},{3,4},{4,3},{5,6},{6,5},{7,8},{8,7},{9,10},{10,9},{11,... | collective-permute-start | bytes 466952 | tf_op jit(solution)/shard_map/ppermute | solution.py:581
  42.3 27.1 %all-to-all-start.1 = ((bf16[16,304,128]{2,1,0:T(8,128)(2,1)}), bf16[16,304,128]{2,1,0:T(8,128)(2,1)}, u32[]{:S(2)}, u32[]{:S(2)}) async-start(bf16[16,304,128]{2,1,0:T(8,128)(2,1)} %get-tuple-element.30), calls=%async_computation.1 | async-start | bytes 2490368 | tf_op jit(solution)/shard_map/all_to_all | solution.py:585
  46.7 19.5 %collective-permute-start.2 = (bf16[2,304,128]{2,1,0:T(8,128)(2,1)}, bf16[2,304,128]{2,1,0:T(8,128)(2,1)}, u32[]{:S(2)}, u32[]{:S(2)}) collective-permute-start(bf16[2,304,128]{2,1,0:T(8,128)(2,1)} %get-tuple-element.28), channel_id=1, source_target_pairs={{0,1},{1,0},{2,3},{3,2},{4,5},{5,4},{6,7},{7,6},{8,9},{9,8},{10,11... | collective-permute-start | bytes 466952 | tf_op jit(solution)/shard_map/ppermute | solution.py:581
  47.9 21.5 %collective-permute-start.3 = (bf16[2,304,128]{2,1,0:T(8,128)(2,1)}, bf16[2,304,128]{2,1,0:T(8,128)(2,1)}, u32[]{:S(2)}, u32[]{:S(2)}) collective-permute-start(bf16[2,304,128]{2,1,0:T(8,128)(2,1)} %get-tuple-element.29), channel_id=1, source_target_pairs={{1,2},{2,1},{3,4},{4,3},{5,6},{6,5},{7,8},{8,7},{9,10},{10,9},{11,... | collective-permute-start | bytes 466952 | tf_op jit(solution)/shard_map/ppermute | solution.py:581

commit v5 on v4

--- a/solution.py
+++ b/solution.py
@@ -391,7 +391,7 @@
             for x in range(8):
                 rows = slice(x * 64, x * 64 + 64)
                 value = whole_plane(part, sums, pair, half, x)
-                value = value / (1.0 + jnp.exp(-value)) * mask[brick, rows, :].astype(jnp.float32)
+                value = value * (0.5 + 0.5 * jnp.tanh(0.5 * value)) * mask[brick, rows, :].astype(jnp.float32)
                 done[brick, rows, :] = value.astype(jnp.bfloat16)
                 planes.append(value)
             store_shell(own.at[brick], planes)

time: 77.2 us -> 77.1 us (level)
  no operation moved by 1% of the time
where the time goes in v5:
time: 77.1 us; the launch traced here: 76.3 us
  Pallas kernels  43.1 us (56%)
  starting transfers between devices  28.1 us (36%)
  waiting for transfers between devices  4.93 us (6%)
    ppermute x4, starting transfers between devices, swapped(): return lax.ppermute(value, axes, routes)  16.7 us
    pallas_call x1, Pallas kernels, first_own(): pl.pallas_call(first_own_kernel, grid=GRID, in_specs=[pair_spec(), WHOLE(...  12.3 us
    all_to_all x2, starting transfers between devices, exchange(): lax.all_to_all(outgoing, 'dev', split_axis=0, concat_axis=0, tiled=True)  11.4 us
    pallas_call x1, Pallas kernels, second_own(): pl.pallas_call(second_own_kernel, grid=GRID, in_specs=[pair_spec(), pair_...  11.3 us
    pallas_call x1, Pallas kernels, first_halo(): pl.pallas_call(first_halo_kernel, in_specs=[SCALARS(), SCALARS(), WHOLE()...  8.17 us
    pallas_call x1, Pallas kernels, second_halo(): pl.pallas_call(second_halo_kernel, in_specs=[SCALARS()] + [ANYWHERE()] *...  7.03 us
    ppermute x4, waiting for transfers between devices, swapped(): return lax.ppermute(value, axes, routes)  4.93 us
    pallas_call x1, Pallas kernels, pack(): pl.pallas_call(pack_kernel, in_specs=[SCALARS(), ANYWHERE(), WHOLE(), ANY...  4.31 us
  transfers between devices with their start and end apart: 6, of which 2 were waited for; matrix products, arithmetic and copies ran while one was open for 0% of the time, Pallas kernels for 31%

profile of v5, /device:TPU:65, one launch (start us, length us, event | category | flops | bytes accessed | tf_op | source)
XLA Modules:
  0.0 76.3 jit_solution(10609789564254113975)
XLA Ops:
  0.0 4.3 %pack_shells.1 = (bf16[16,304,128]{2,1,0:T(8,128)(2,1)}, bf16[2,304,128]{2,1,0:T(8,128)(2,1)}, bf16[2,304,128]{2,1,0:T(8,128)(2,1)}) custom-call(s32[16]{0:T(128)} %bitcast.1, bf16[12,512,128]{2,1,0:T(8,128)(2,1)} %feat_ref.3, s32[12,512]{1,0:T(8,128)} %occ_ref.3, bf16[304,512]{1,0:T(8,128)(2,1)} %constant.2.clone.pick_ref), custom_call_target="tpu_custom_call" | custom-call | tf_op jit(solution)/shard_map/pack_shells/pallas_call | solution.py:505
  4.3 7.0 %all-to-all-start = ((bf16[16,304,128]{2,1,0:T(8,128)(2,1)}), bf16[16,304,128]{2,1,0:T(8,128)(2,1)}, u32[]{:S(2)}, u32[]{:S(2)}) async-start(bf16[16,304,128]{2,1,0:T(8,128)(2,1)} %get-tuple-element.23), calls=%async_computation | async-start | bytes 2490368 | tf_op jit(solution)/shard_map/all_to_all | solution.py:585
  11.3 1.3 %collective-permute-start = (bf16[2,304,128]{2,1,0:T(8,128)(2,1)}, bf16[2,304,128]{2,1,0:T(8,128)(2,1)}, u32[]{:S(2)}, u32[]{:S(2)}) collective-permute-start(bf16[2,304,128]{2,1,0:T(8,128)(2,1)} %get-tuple-element.21), channel_id=1, source_target_pairs={{0,1},{1,0},{2,3},{3,2},{4,5},{5,4},{6,7},{7,6},{8,9},{9,8},{10,11... | collective-permute-start | bytes 466952 | tf_op jit(solution)/shard_map/ppermute | solution.py:581
  12.6 7.1 %collective-permute-start.1 = (bf16[2,304,128]{2,1,0:T(8,128)(2,1)}, bf16[2,304,128]{2,1,0:T(8,128)(2,1)}, u32[]{:S(2)}, u32[]{:S(2)}) collective-permute-start(bf16[2,304,128]{2,1,0:T(8,128)(2,1)} %get-tuple-element.22), channel_id=1, source_target_pairs={{1,2},{2,1},{3,4},{4,3},{5,6},{6,5},{7,8},{8,7},{9,10},{10,9},{11,... | collective-permute-start | bytes 466952 | tf_op jit(solution)/shard_map/ppermute | solution.py:581
  19.7 12.3 %first_own.1 = (f32[6,512,256]{2,1,0:T(8,128)}, bf16[12,512,128]{2,1,0:T(8,128)(2,1)}, bf16[12,512,128]{2,1,0:T(8,128)(2,1)}, bf16[12,304,128]{2,1,0:T(8,128)(2,1)}) custom-call(bf16[12,512,128]{2,1,0:T(8,128)(2,1)} %feat_ref.3, s32[12,512]{1,0:T(8,128)} %occ_ref.3, bf16[27,128,128]{2,1,0:T(8,128)(2,1)} %w_ref.5), custom_call_target="tpu_custom_call" | custom-call | flops 7247757312 | bytes 8388608 | tf_op jit(solution)/shard_map/first_own/pallas_call | solution.py:523
  32.0 0.0 collective-permute-done.near_in_ref
  32.0 1.9 %collective-permute-done.1.far_in_ref = bf16[2,304,128]{2,1,0:T(8,128)(2,1)} collective-permute-done((bf16[2,304,128]{2,1,0:T(8,128)(2,1)}, bf16[2,304,128]{2,1,0:T(8,128)(2,1)}, u32[]{:S(2)}, u32[]{:S(2)}) %collective-permute-start.1) | collective-permute-done | bytes 155680 | tf_op jit(solution)/shard_map/ppermute | solution.py:581
  33.9 0.0 all-to-all-done.recv_ref
  33.9 8.2 %first_halo.1 = (bf16[12,512,128]{2,1,0:T(8,128)(2,1)}, bf16[16,304,128]{2,1,0:T(8,128)(2,1)}, bf16[2,304,128]{2,1,0:T(8,128)(2,1)}, bf16[2,304,128]{2,1,0:T(8,128)(2,1)}) custom-call(s32[12,27]{1,0:T(8,128)} %src_ref.3, s32[16]{0:T(128)} %bitcast.2, bf16[80,512]{1,0:T(8,128)(2,1)} %constant.7.pick_ref, f32[6,512,256]{2,1,0:T(8,128)} %get-tuple-element.18.part_ref, ...), custom_call_target="tpu_custom_call" | custom-call | flops 1811939328 | bytes 10485760 | tf_op jit(solution)/shard_map/first_halo/pallas_call | solution.py:551
  42.1 4.4 %all-to-all-start.1 = ((bf16[16,304,128]{2,1,0:T(8,128)(2,1)}), bf16[16,304,128]{2,1,0:T(8,128)(2,1)}, u32[]{:S(2)}, u32[]{:S(2)}) async-start(bf16[16,304,128]{2,1,0:T(8,128)(2,1)} %get-tuple-element.30), calls=%async_computation.1 | async-start | bytes 2490368 | tf_op jit(solution)/shard_map/all_to_all | solution.py:585
  46.5 1.2 %collective-permute-start.2 = (bf16[2,304,128]{2,1,0:T(8,128)(2,1)}, bf16[2,304,128]{2,1,0:T(8,128)(2,1)}, u32[]{:S(2)}, u32[]{:S(2)}) collective-permute-start(bf16[2,304,128]{2,1,0:T(8,128)(2,1)} %get-tuple-element.28), channel_id=1, source_target_pairs={{0,1},{1,0},{2,3},{3,2},{4,5},{5,4},{6,7},{7,6},{8,9},{9,8},{10,11... | collective-permute-start | bytes 466952 | tf_op jit(solution)/shard_map/ppermute | solution.py:581
  47.7 7.1 %collective-permute-start.3 = (bf16[2,304,128]{2,1,0:T(8,128)(2,1)}, bf16[2,304,128]{2,1,0:T(8,128)(2,1)}, u32[]{:S(2)}, u32[]{:S(2)}) collective-permute-start(bf16[2,304,128]{2,1,0:T(8,128)(2,1)} %get-tuple-element.29), channel_id=1, source_target_pairs={{1,2},{2,1},{3,4},{4,3},{5,6},{6,5},{7,8},{8,7},{9,10},{10,9},{11,... | collective-permute-start | bytes 466952 | tf_op jit(solution)/shard_map/ppermute | solution.py:581
  54.8 11.3 %second_own.1 = (f32[6,512,256]{2,1,0:T(8,128)}, bf16[12,304,128]{2,1,0:T(8,128)(2,1)}) custom-call(bf16[12,512,128]{2,1,0:T(8,128)(2,1)} %get-tuple-element.24.hidden_ref, bf16[12,512,128]{2,1,0:T(8,128)(2,1)} %get-tuple-element.25.x_ref, bf16[27,128,128]{2,1,0:T(8,128)(2,1)} %w_ref.7), custom_call_target="tpu_custom_call" | custom-call | flops 7247757312 | bytes 8388608 | tf_op jit(solution)/shard_map/second_own/pallas_call | solution.py:537
  66.1 0.0 collective-permute-done.2.near_in_ref
  66.1 3.1 %collective-permute-done.3.far_in_ref = bf16[2,304,128]{2,1,0:T(8,128)(2,1)} collective-permute-done((bf16[2,304,128]{2,1,0:T(8,128)(2,1)}, bf16[2,304,128]{2,1,0:T(8,128)(2,1)}, u32[]{:S(2)}, u32[]{:S(2)}) %collective-permute-start.3) | collective-permute-done | bytes 155680 | tf_op jit(solution)/shard_map/ppermute | solution.py:581
  69.2 0.0 all-to-all-done.1.recv_ref
  69.2 7.0 %second_halo.1 = bf16[12,512,128]{2,1,0:T(8,128)(2,1)} custom-call(s32[12,27]{1,0:T(8,128)} %src_ref.3, f32[6,512,256]{2,1,0:T(8,128)} %get-tuple-element.26.part_ref, bf16[12,512,128]{2,1,0:T(8,128)(2,1)} %get-tuple-element.19.mask_ref, bf16[27,128,128]{2,1,0:T(8,128)(2,1)} %w_ref.7, bf16[12,304,128]{2,1,0:T(8,128)(2,1)} %get-tuple-element.27.shells_ref, ...), custom_call_target="tpu_custom_call" | custom-call | flops 1811939328 | bytes 10485760 | tf_op jit(solution)/shard_map/second_halo/pallas_call | solution.py:564
Async XLA Ops:
  4.3 29.6 %all-to-all-start = ((bf16[16,304,128]{2,1,0:T(8,128)(2,1)}), bf16[16,304,128]{2,1,0:T(8,128)(2,1)}, u32[]{:S(2)}, u32[]{:S(2)}) async-start(bf16[16,304,128]{2,1,0:T(8,128)(2,1)} %get-tuple-element.23), calls=%async_computation | async-start | bytes 2490368 | tf_op jit(solution)/shard_map/all_to_all | solution.py:585
  11.3 20.7 %collective-permute-start = (bf16[2,304,128]{2,1,0:T(8,128)(2,1)}, bf16[2,304,128]{2,1,0:T(8,128)(2,1)}, u32[]{:S(2)}, u32[]{:S(2)}) collective-permute-start(bf16[2,304,128]{2,1,0:T(8,128)(2,1)} %get-tuple-element.21), channel_id=1, source_target_pairs={{0,1},{1,0},{2,3},{3,2},{4,5},{5,4},{6,7},{7,6},{8,9},{9,8},{10,11... | collective-permute-start | bytes 466952 | tf_op jit(solution)/shard_map/ppermute | solution.py:581
  12.6 21.3 %collective-permute-start.1 = (bf16[2,304,128]{2,1,0:T(8,128)(2,1)}, bf16[2,304,128]{2,1,0:T(8,128)(2,1)}, u32[]{:S(2)}, u32[]{:S(2)}) collective-permute-start(bf16[2,304,128]{2,1,0:T(8,128)(2,1)} %get-tuple-element.22), channel_id=1, source_target_pairs={{1,2},{2,1},{3,4},{4,3},{5,6},{6,5},{7,8},{8,7},{9,10},{10,9},{11,... | collective-permute-start | bytes 466952 | tf_op jit(solution)/shard_map/ppermute | solution.py:581
  42.1 27.1 %all-to-all-start.1 = ((bf16[16,304,128]{2,1,0:T(8,128)(2,1)}), bf16[16,304,128]{2,1,0:T(8,128)(2,1)}, u32[]{:S(2)}, u32[]{:S(2)}) async-start(bf16[16,304,128]{2,1,0:T(8,128)(2,1)} %get-tuple-element.30), calls=%async_computation.1 | async-start | bytes 2490368 | tf_op jit(solution)/shard_map/all_to_all | solution.py:585
  46.5 19.6 %collective-permute-start.2 = (bf16[2,304,128]{2,1,0:T(8,128)(2,1)}, bf16[2,304,128]{2,1,0:T(8,128)(2,1)}, u32[]{:S(2)}, u32[]{:S(2)}) collective-permute-start(bf16[2,304,128]{2,1,0:T(8,128)(2,1)} %get-tuple-element.28), channel_id=1, source_target_pairs={{0,1},{1,0},{2,3},{3,2},{4,5},{5,4},{6,7},{7,6},{8,9},{9,8},{10,11... | collective-permute-start | bytes 466952 | tf_op jit(solution)/shard_map/ppermute | solution.py:581
  47.7 21.5 %collective-permute-start.3 = (bf16[2,304,128]{2,1,0:T(8,128)(2,1)}, bf16[2,304,128]{2,1,0:T(8,128)(2,1)}, u32[]{:S(2)}, u32[]{:S(2)}) collective-permute-start(bf16[2,304,128]{2,1,0:T(8,128)(2,1)} %get-tuple-element.29), channel_id=1, source_target_pairs={{1,2},{2,1},{3,4},{4,3},{5,6},{6,5},{7,8},{8,7},{9,10},{10,9},{11,... | collective-permute-start | bytes 466952 | tf_op jit(solution)/shard_map/ppermute | solution.py:581
